TPU v7x, 32 devices: a whole 2x2x4 slice. The times are simulated.
32 devices in a mesh: lat: 8 (over y, x, core), lon: 4 (over z).
Axes of the slice: x: 2, y: 2, z: 4, core: 2. Of those that a mesh axis runs over, the one named last changes fastest.
Arguments:
- tokens: bfloat16 [2, 96, 96, 512], P(None, 'lat', 'lon'), may hold values from -48 to 48
- region_ids: int32 [2, 96, 96], replicated, may hold values from 0 to 3
- shifts: int32 [2], replicated, may hold values from 1 to 5, as said below
- fine_qkv: bfloat16 [512, 1536], replicated, may hold values from -2 to 2
- fine_proj: bfloat16 [512, 512], replicated, may hold values from -0.25 to 0.25
- merge_weight: bfloat16 [2048, 1024], replicated, may hold values from -0.125 to 0.125
- coarse_qkv: bfloat16 [1024, 1536], replicated, may hold values from -0.1875 to 0.1875
- coarse_proj: bfloat16 [512, 1024], replicated, may hold values from -0.25 to 0.25
Outputs:
- fine_out: bfloat16 [2, 96, 96, 512], P(None, 'lat', 'lon')
- coarse_out: bfloat16 [2, 48, 48, 1024], P(None, 'lat', 'lon')
Inputs may be any that keep to these rules, and one draw needn't show every extreme that they name: `shifts`: entry 0 is the fine level's shift, entry 1 the coarse level's; one of them is 5.
All inputs are finite; a program needn't handle non-finite values.
Results may differ from a plain program's by a relative error of at most 0.012.
The roundings to bfloat16 on the way count: a program that leaves them out, or rounds other values in their place, can miss the bound.
Values may be sent and summed in bfloat16 or wider, within the bound.
No kernel may reach another device: no remote copies, remote signals or barrier semaphores. Data moves between devices by JAX's collectives and lax.ppermute only.
A program may use at most 128 MiB of HBM per device.

v0:
```python
import functools

import jax
import jax.numpy as jnp
import numpy as np
from jax import lax
from jax.experimental import pallas as pl
from jax.experimental.pallas import tpu as pltpu
from jax.sharding import PartitionSpec as P

HD = 32
WH = 6
WW = 12
TOK = 2 * WH * WW
EPS = 1e-05
BIG = 1e30
SCALE = float(np.log2(np.e) / np.sqrt(HD))

NT = (((1,), (1,)), ((), ()))
TN = (((0,), (0,)), ((), ()))
F32 = jnp.float32
BF16 = jnp.bfloat16
I32 = jnp.int32

PAIRS = [(WH - 1, t) for t in range(1, WH)] + [(t, WH - 1) for t in range(1, WH - 1)]


def up16(count):
    return -(-count // 16) * 16


def natural(rows, cols):
    return [(l, r, c) for l in range(2) for r in range(rows) for c in range(cols)]


def windowed(rows, cols):
    return [
        (l, wr * WH + r, wc * WW + c)
        for wr in range(rows // WH)
        for wc in range(cols // WW)
        for l in range(2)
        for r in range(WH)
        for c in range(WW)
    ]


def moved(order, d):
    return [(l, r + d, c + 2 * d) for l, r, c in order]


def exchange_places(held, wanted, rows, cols, sign):
    at = {place: n for n, place in enumerate(held)}
    found = []
    for dr, dc in ((sign, 0), (0, sign), (sign, sign)):
        numbers, places = [], []
        for l, r, c in sorted(set(wanted) - set(held)):
            n = at.get((l, r - dr * rows, c - dc * cols))
            if n is not None:
                numbers.append(n)
                places.append((l, r, c))
        found.append((numbers, places))
    return found


def offsets(t0, t1):
    a = t0 if t0 <= 2 else t0 - WH
    big_a = t1 if t1 <= 2 else t1 - WH
    ahead = 1 if 2 * big_a > a or 2 * big_a - a == 0 and a < 0 else -1
    return a, big_a, ahead


def classes_of(needs, slack):
    rounded = [tuple(-(-size // 8) * 8 for size in need) for need in needs]
    heavy = [sum(need[1:3]) * 2 + sum(need[4:]) for need in rounded]
    limits = []
    for size in sorted(set(heavy)):
        if not limits or size > limits[-1][0] * slack:
            limits.append([size, size])
        limits[-1][1] = size
    which = [next(n for n, limit in enumerate(limits) if size <= limit[1]) for size in heavy]
    sizes = [
        [max(need[k] for need, w in zip(rounded, which) if w == n) for k in range(len(needs[0]))]
        for n in range(len(limits))
    ]
    return sizes, which


def rooms(sizes):
    return [up16(max(size[k] for size in sizes)) for k in range(len(sizes[0]))]


class Plan:
    def __init__(self, rows, cols):
        crows, ccols = rows // 2, cols // 2
        block, cblock = natural(rows, cols), natural(crows, ccols)
        cases = []
        for t0, t1 in PAIRS:
            a, big_a, ahead = offsets(t0, t1)
            fine = moved(windowed(rows, cols), a)
            coarse = moved(cblock, big_a)
            quarters = [
                (l, 2 * r + dr, 2 * c + dc)
                for dr, dc in ((0, 0), (1, 0), (0, 1), (1, 1))
                for l, r, c in coarse
            ]
            come = 1 if a > 0 else -1
            one = exchange_places(block, fine, rows, cols, come)
            home = [p for p in block if p not in set(fine)]
            wanted = quarters + (home if come == -ahead and 2 * big_a != a else [])
            two = exchange_places(fine, wanted, rows, cols, ahead)
            back = 1 if big_a < 0 else -1
            three = exchange_places(coarse, cblock, crows, ccols, back)
            got = set(fine).union(*[places for _, places in two])
            four = exchange_places(fine, [p for p in block if p not in got], rows, cols, back)
            cases.append((come, ahead, back, fine, coarse, quarters, one, two, three, four))

        def needs(which):
            return [[len(numbers) for numbers, _ in case[which]] for case in cases]

        self.one, one_class = classes_of(needs(6), 1.15)
        self.two, two_class = classes_of(needs(7), 1.15)
        sizes, three_class = classes_of([three + four for three, four in zip(needs(8), needs(9))], 1.0)
        self.three, self.four = [size[:3] for size in sizes], [size[3:] for size in sizes]
        self.room_one, self.room_two = rooms(self.one), rooms(self.two)
        self.room_three, self.room_four = rooms(self.three), rooms(self.four)

        def branches(which_class, direction):
            pairs = [(n, case[direction]) for n, case in zip(which_class, cases)]
            found = sorted(set(pairs))
            return found, [found.index(pair) for pair in pairs]

        self.one_branches, one_at = branches(one_class, 0)
        self.two_branches, two_at = branches(two_class, 1)
        self.three_branches, three_at = branches(three_class, 2)
        self.flags = dict(
            three_class=three_class,
            one_at=one_at, two_at=two_at, three_at=three_at,
            a=[offsets(*pair)[0] for pair in PAIRS], big_a=[offsets(*pair)[1] for pair in PAIRS],
        )

        found = {}
        for n, (come, ahead, back, fine, coarse, quarters, one, two, three, four) in enumerate(cases):

            def send(exchanged, room):
                return [n for (numbers, _), size in zip(exchanged, room) for n in numbers + [-1] * (size - len(numbers))]

            def source(held, *exchanges):
                places = list(held)
                for exchanged, room in exchanges:
                    for (_, got), size in zip(exchanged, room):
                        places += got + [None] * (size - len(got))
                return {p: n for n, p in enumerate(places) if p is not None}

            first, second = source(block, (one, self.room_one)), source(fine, (two, self.room_two))
            third = source(coarse, (three, self.room_three))
            last = source(fine, (two, self.room_two), (four, self.room_four))
            out = [(l, r, c) for r in range(crows) for c in range(ccols) for l in range(2)]
            rows_of = dict(
                send_one=send(one, self.room_one),
                take_one=[first[p] for p in fine],
                send_two=send(two, self.room_two),
                take_two=[second[p] for p in quarters],
                send_three=send(three, self.room_three),
                send_four=send(four, self.room_four),
                fine_out=[last[p] for p in block],
                coarse_out=[third[p] for p in out],
            )
            for name, row in rows_of.items():
                found.setdefault(name, []).append(row)
        parts, self.at, top = [], {}, 0
        for name, lists in found.items():
            length = -(-max(len(row) for row in lists) // 128)
            part = np.full((len(PAIRS), length * 128), -1, np.float32)
            for n, row in enumerate(lists):
                part[n, : len(row)] = row
            parts.append(part.reshape(len(PAIRS), length, 128))
            self.at[name] = (top, length)
            top += length
        parts.append(np.zeros((len(PAIRS), -top % 8, 128), np.float32))
        self.table = np.concatenate(parts, axis=1)


def case_of(shifts_ref):
    t0, t1 = shifts_ref[0], shifts_ref[1]
    return jnp.where(t0 == WH - 1, t1 - 1, t0 + WH - 2)


def lookup(values, case):
    out = jnp.int32(values[0])
    for n, value in enumerate(values[1:], 1):
        out = jnp.where(case == n, value, out)
    return out


def columns_of(rows, count):
    parts = [jnp.broadcast_to(rows[j : j + 1], (128, 128)).T for j in range(-(-count // 128))]
    return stack_rows(parts)[:count]


def select_rows(index, source):
    lane = lax.broadcasted_iota(I32, (1, 128), 1).astype(F32)
    size = source.shape[0]
    pick = [jnp.where(index == lane + float(at), 1.0, 0.0).astype(BF16) for at in range(0, size, 128)]
    pick = jnp.concatenate(pick, axis=1)[:, :size]
    return jnp.dot(pick, source, preferred_element_type=F32)


def stack_rows(parts):
    return parts[0] if len(parts) == 1 else jnp.concatenate(parts, axis=0)


def layer_norm(values):
    center = jnp.mean(values, axis=-1, keepdims=True)
    values = values - center
    spread = jnp.mean(values * values, axis=-1, keepdims=True)
    return values * lax.rsqrt(spread + EPS)


def attend_windows(qkv_of, id_of, windows, inner, finish):
    lane = lax.broadcasted_iota(I32, (1, 128), 1)
    forbid = jnp.where(lane < 8, BIG, 0.0).astype(BF16)
    groups = inner // 128
    units = [(w, g) for w in range(windows) for g in range(groups)]
    scores, weights, outs = {}, {}, {}

    def score(w, g):
        key_id = id_of(w)
        not_id = (key_id - 1).astype(BF16) * forbid
        q = qkv_of(w, g * 128)
        keys = jnp.concatenate([qkv_of(w, inner + g * 128), key_id], axis=1)
        queries = []
        for h in range(4):
            mine = jnp.where((lane >= h * HD) & (lane < (h + 1) * HD), 1.0, 0.0).astype(BF16)
            queries.append(jnp.concatenate([q * mine, not_id], axis=1))
        scores[w, g] = lax.dot_general(stack_rows(queries), keys, NT, preferred_element_type=F32)

    def soften(w, g):
        s = scores.pop((w, g))
        weights[w, g] = jnp.exp2((s - jnp.max(s, axis=1, keepdims=True)) * SCALE).astype(BF16)

    def gather(w, g):
        v = qkv_of(w, 2 * inner + g * 128)
        values = jnp.concatenate([v, jnp.ones_like(v)], axis=1)
        out = jnp.dot(weights.pop((w, g)), values, preferred_element_type=F32)
        picked, total = out[:TOK, :128], out[:TOK, 128:]
        for h in range(1, 4):
            rows = slice(h * TOK, (h + 1) * TOK)
            picked = jnp.where(lane < h * HD, picked, out[rows, :128])
            total = jnp.where(lane < h * HD, total, out[rows, 128:])
        outs[w, g] = (picked / total).astype(BF16)
        if g == groups - 1:
            finish(w, jnp.concatenate([outs.pop((w, k)) for k in range(groups)], axis=1))

    for n in range(len(units) + 2):
        if n < len(units):
            score(*units[n])
        if 0 <= n - 1 < len(units):
            soften(*units[n - 1])
        if 0 <= n - 2 < len(units):
            gather(*units[n - 2])


ANY = pl.BlockSpec(memory_space=pl.ANY)
HBM = pl.BlockSpec(memory_space=pltpu.HBM)
VMEM = pl.BlockSpec(memory_space=pltpu.VMEM)
SMEM = pl.BlockSpec(memory_space=pltpu.SMEM)


def call(body, outs, args, in_specs, scratch, copies, flops, moved_bytes, vmem=8):
    args = [
        pltpu.with_memory_space_constraint(arg, spec.memory_space) for arg, spec in zip(args, in_specs, strict=True)
    ]
    spaces = [getattr(out, "memory_space", pltpu.SMEM if out.dtype == I32 else pltpu.VMEM) for out in outs]
    out_specs = [pl.BlockSpec(memory_space=space) for space in spaces]
    return pl.pallas_call(
        body,
        out_shape=outs,
        in_specs=in_specs,
        out_specs=out_specs,
        scratch_shapes=list(scratch) + [pltpu.SemaphoreType.DMA((copies,))],
        compiler_params=pltpu.CompilerParams(vmem_limit_bytes=vmem << 20),
        cost_estimate=pl.CostEstimate(flops=flops, bytes_accessed=moved_bytes, transcendentals=0),
    )(*args)


def shapes(sizes, width, space=pltpu.VMEM):
    return [space((n, width), BF16) for n in sizes]


class Copies:
    def __init__(self, sems):
        self.sems, self.used = sems, 0

    def __call__(self, src, dst):
        copy = pltpu.make_async_copy(src, dst, self.sems.at[self.used])
        self.used += 1
        copy.start()
        return copy


def lay(pieces, room):
    pieces = [piece for piece in pieces if piece is not None]
    if not pieces:
        return None
    width = pieces[0].shape[1]

    def body(*refs):
        out_ref = refs[len(pieces)]
        at = 0
        for ref, space in zip(refs, room):
            rows = ref.shape[0]
            out_ref[at : at + rows, :] = ref[...]
            if rows < space:
                out_ref[at + rows : at + space, :] = jnp.zeros((space - rows, width), BF16)
            at += space

    return call(body, shapes([sum(room)], width), pieces, [VMEM] * 3, [], 1, 0, 1 << 18)[0]


def zeros(shape):
    def body(out_ref, _):
        out_ref[...] = jnp.zeros(shape, BF16)

    return call(body, [pltpu.VMEM(shape, BF16)], [], [], [], 1, 0, 1 << 18)[0]


def flat(ref):
    layers, rows, cols, width = ref.shape
    return ref[...].astype(F32).reshape(layers * rows * cols, width).astype(BF16)


def put_pieces(value, refs):
    at = 0
    for ref in refs:
        ref[...] = value[at : at + ref.shape[0]].astype(BF16)
        at += ref.shape[0]


def rows_of(plan, table_ref, name, *lead):
    top, length = plan.at[name]
    return table_ref[(*lead, slice(top, top + length), slice(None))]


def exchange(pieces, sizes, sign):
    if not any(sizes):
        return [None] * 3
    lat, lon = lax.axis_size("lat"), lax.axis_size("lon")
    row, col, both = [piece[:size] for piece, size in zip(pieces, sizes)]
    pairs = [((i + sign) % lat * lon + (j + sign) % lon, i * lon + j) for i in range(lat) for j in range(lon)]
    col = lax.ppermute(col, "lon", [((j + sign) % lon, j) for j in range(lon)])
    both = lax.ppermute(both, ("lat", "lon"), pairs)
    row = lax.ppermute(row, "lat", [((i + sign) % lat, i) for i in range(lat)])
    return [row, col, both]


def choose(index, branches, *args):
    flat_args, tree = jax.tree.flatten(args)
    out_trees = []

    def closed(branch):
        def run(*leaves):
            out, out_tree = jax.tree.flatten(branch(*jax.tree.unflatten(tree, leaves)))
            out_trees.append(out_tree)
            return out

        return jax.make_jaxpr(run)(*flat_args)

    out = lax.cond_p.bind(index, *flat_args, branches=tuple(closed(branch) for branch in branches))
    return jax.tree.unflatten(out_trees[0], out)


FLAGS = ("three_class", "a", "big_a")


def first_pieces(shifts, tokens, plan):
    width = tokens.shape[-1]
    count = tokens.size // width
    kinds = 3

    def body(shifts_hbm, tokens_hbm, table_hbm, *refs):
        outs, refs = refs[:kinds], refs[kinds:]
        source_ref, rows_ref, flags_ref, *at_refs, shifts_ref, tokens_ref, table_ref, sems = refs
        start = Copies(sems)
        shift = start(shifts_hbm, shifts_ref)
        held = start(tokens_hbm, tokens_ref)
        table = start(table_hbm, table_ref)
        shift.wait()
        case = case_of(shifts_ref)
        for ref, name in zip(at_refs, ("one_at", "two_at", "three_at")):
            ref[0] = lookup(plan.flags[name], case)
        for n, name in enumerate(FLAGS):
            flags_ref[n] = lookup(plan.flags[name], case)
        held.wait()
        source_ref[...] = flat(tokens_ref)
        table.wait()
        rows_ref[...] = table_ref[case]
        index = columns_of(rows_of(plan, table_ref, "send_one", case), sum(plan.room_one))
        put_pieces(select_rows(index, source_ref[...]), outs)

    outs = shapes([*plan.room_one, count], width)
    outs += [pltpu.VMEM(plan.table.shape[1:], F32), pltpu.SMEM((8,), I32)]
    outs += [pltpu.SMEM((1,), I32)] * 3
    scratch = [pltpu.SMEM((2,), I32), pltpu.VMEM(tokens.shape, BF16), pltpu.VMEM(plan.table.shape, F32)]
    got = call(body, outs, [shifts, tokens, plan.table], [HBM] * 3, scratch, 3, 1 << 28, 1 << 20)
    sent, (source, rows, flags, one, two, three) = got[:kinds], got[kinds:]
    return sent, source, rows, flags, one[0], two[0], three[0]


def before_fine(flags, regions, tokens, table, weights, plan, rows, cols):
    _, lat, lon = regions.shape
    width = tokens.shape[1]
    flat_regions = regions.reshape(2 * lat, lon)
    fine, coarse = windowed(rows, cols), natural(rows // 2, cols // 2)

    def lanes(places, scale, is_fine):
        places = np.asarray([(l, scale * r, scale * c, is_fine) for l, r, c in places], np.float32)
        return np.pad(places, ((0, -len(places) % 128), (0, 0))).T.reshape(4, -1, 128)

    places = np.concatenate([lanes(fine, 1, 1), lanes(coarse, 2, 0)], axis=1)
    lines = places.shape[1]

    def body(flags_ref, rows_ref, tokens_ref, regions_hbm, places_hbm, *refs):
        weights_hbm, refs = refs[: len(weights)], refs[len(weights) :]
        id_ref, x_ref, *refs = refs
        weight_refs, (regions_ref, places_ref, sems) = refs[: len(weights)], refs[len(weights) :]
        start = Copies(sems)
        waits = [start(regions_hbm, regions_ref), start(places_hbm, places_ref)]
        later = [
            start(src.at[:, pl.ds(0, dst.shape[1])], dst) for src, dst in zip(weights_hbm, weight_refs)
        ]
        for copy in waits:
            copy.wait()
        a = flags_ref[1].astype(F32)
        big_a = 2.0 * flags_ref[2].astype(F32)
        is_fine = places_ref[3]
        d = is_fine * a + (1.0 - is_fine) * big_a
        row = places_ref[1] + d + (lax.axis_index("lat") * rows).astype(F32)
        col = places_ref[2] + 2.0 * d + (lax.axis_index("lon") * cols).astype(F32)
        wrapped = jnp.where((row < 0) | (row >= lat), 4.0, 0.0)
        row = jnp.where(row < 0, row + lat, jnp.where(row >= lat, row - lat, row))
        col = jnp.where(col < 0, col + lon, jnp.where(col >= lon, col - lon, col))
        row = row + places_ref[0] * lat

        def along(values):
            return jnp.concatenate([values[n : n + 1] for n in range(lines)], axis=1)

        line = lax.broadcasted_iota(I32, (2 * lat, 1), 0).astype(F32)
        pick = jnp.where(line == along(row), 1.0, 0.0).astype(BF16)
        known = regions_ref[...].astype(F32).astype(BF16)
        picked = lax.dot_general(known, pick, TN, preferred_element_type=F32)
        line = lax.broadcasted_iota(I32, (lon, 1), 0).astype(F32)
        ids = jnp.sum(jnp.where(line == along(col), picked, 0.0), axis=0, keepdims=True) + along(wrapped)
        for n in range(lines):
            id_ref[n : n + 1, :] = ids[:, n * 128 : (n + 1) * 128]
        take = columns_of(rows_of(plan, rows_ref, "take_one"), len(fine))
        x_ref[...] = select_rows(take, tokens_ref[...]).astype(BF16)
        for copy in later:
            copy.wait()

    outs = [pltpu.VMEM((lines, 128), F32)] + shapes([len(fine)], width)
    outs += [pltpu.VMEM((w.shape[0], min(w.shape[1], 2 * weights[1].shape[0])), BF16) for w in weights]
    scratch = [pltpu.VMEM(flat_regions.shape, I32), pltpu.VMEM(places.shape, F32)]
    args = [flags, table, tokens, flat_regions, places, *weights]
    in_specs = [SMEM, VMEM, VMEM] + [HBM] * (2 + len(weights))
    ids, x, *weights = call(body, outs, args, in_specs, scratch, 2 + len(weights), 1 << 28, 4 << 20)
    return ids, x, weights


def id_columns(lines, count):
    lane = lax.broadcasted_iota(I32, (1, 128), 1).astype(F32)
    return jnp.where(columns_of(lines, count) == lane, 1.0, 0.0).astype(BF16)


def before_coarse(flags, fine, table, weight, plan):
    own, width = fine.shape
    half = 9 * weight.shape[0] // 32

    def body(flags_ref, rows_ref, fine_ref, weight_hbm, x_ref, part_hbm, home_ref, weight_ref, part_ref, sems):
        start = Copies(sems)
        later = start(weight_hbm.at[pl.ds(0, half)], weight_ref)
        take = columns_of(rows_of(plan, rows_ref, "fine_out"), own)
        part_ref[...] = select_rows(take, fine_ref[...]).astype(BF16)
        leave = start(part_ref, part_hbm)
        take = columns_of(rows_of(plan, rows_ref, "take_two"), own)
        x_ref[...] = select_rows(take, fine_ref[...]).astype(BF16)

        @pl.when(needs_fine(flags_ref, plan))
        def _():
            index = columns_of(rows_of(plan, rows_ref, "send_four"), sum(plan.room_four))
            home_ref[...] = select_rows(index, fine_ref[...]).astype(BF16)

        leave.wait()
        later.wait()

    outs = shapes([own], width) + shapes([own], width, pltpu.HBM)
    outs += shapes([sum(plan.room_four)], width) + shapes([half], weight.shape[1])
    scratch = [pltpu.VMEM(fine.shape, BF16)]
    args = [flags, table, fine, weight]
    return call(body, outs, args, [SMEM, VMEM, VMEM, HBM], scratch, 2, 1 << 28, 4 << 20)


def needs_fine(flags_ref, plan):
    with_fine = [n for n, sizes in enumerate(plan.four) if sum(sizes)]
    return functools.reduce(jnp.logical_or, [flags_ref[0] == n for n in with_fine])


def fine_level(x_own, source, ids, w_qk, w_proj, w_qkv, rows, plan):
    count, width = x_own.shape
    inner = w_proj.shape[0]

    def body(own_ref, source_ref, ids_ref, qk_w_ref, proj_w_ref, qkv_w_hbm, rows_ref, out_ref, *refs):
        *piece_outs, x_ref, qkv_ref, id_ref, v_w_ref, sems = refs
        v_w = Copies(sems)(qkv_w_hbm.at[:, pl.ds(2 * inner, inner)], v_w_ref)
        id_ref[...] = id_columns(ids_ref[: -(-count // 128), :], count)
        take = columns_of(rows_of(plan, rows_ref, "take_one"), count) - float(count)
        x = own_ref[...].astype(F32) + select_rows(take, source_ref[...])
        x_ref[...] = x
        normed = layer_norm(x).astype(BF16)
        v_w.wait()
        qkv_ref[:, : 2 * inner] = jnp.dot(normed, qk_w_ref[...], preferred_element_type=F32).astype(BF16)
        qkv_ref[:, 2 * inner :] = jnp.dot(normed, v_w_ref[...], preferred_element_type=F32).astype(BF16)

        def finish(w, out):
            at = slice(w * TOK, (w + 1) * TOK)
            out = jnp.dot(out, proj_w_ref[...], preferred_element_type=F32)
            out_ref[at, :] = (x_ref[at, :] + out).astype(BF16)

        attend_windows(
            lambda w, at: qkv_ref[w * TOK : (w + 1) * TOK, at : at + 128],
            lambda w: id_ref[w * TOK : (w + 1) * TOK, :],
            count // TOK,
            inner,
            finish,
        )
        index = columns_of(rows_of(plan, rows_ref, "send_two"), sum(plan.room_two))
        put_pieces(select_rows(index, out_ref[...]), piece_outs)

    outs = shapes([count, *plan.room_two], width)
    scratch = [
        pltpu.VMEM((count, width), F32),
        pltpu.VMEM((count, 3 * inner), BF16),
        pltpu.VMEM((count, 128), BF16),
        pltpu.VMEM((width, inner), BF16),
    ]
    args = [x_own, source, ids, w_qk, w_proj, w_qkv, rows]
    out, *sent = call(body, outs, args, [VMEM] * 5 + [HBM, VMEM], scratch, 1, 3 << 30, 6 << 20, 14)
    return out, sent


def coarse_level(flags, home, x_own, source, ids, merge_first, w_merge, w_qkv, w_proj, rows, plan):
    depth, width = w_merge.shape
    own, half = x_own.shape
    count = own // 4
    inner = w_proj.shape[0]

    def body(
        flags_ref, merge_hbm, qkv_w_hbm, proj_w_hbm, home_ref, own_ref, source_ref, ids_ref, first_ref, rows_ref, *refs
    ):
        out_ref, *piece_outs = refs[:4]
        qkv_ref, id_ref, merge_ref, qkv_w_ref, proj_w_ref, sems = refs[4:]
        start = Copies(sems)
        here = first_ref.shape[0]
        merge_w = start(merge_hbm.at[pl.ds(here, depth - here)], merge_ref)
        qkv_w = start(qkv_w_hbm, qkv_w_ref)
        proj_w = start(proj_w_hbm, proj_w_ref)
        id_ref[...] = id_columns(ids_ref[-(-own // 128) :, :], count)
        take = columns_of(rows_of(plan, rows_ref, "take_two"), 4 * count) - float(own)
        x = own_ref[...].astype(F32) + select_rows(take, source_ref[...])
        x = jnp.concatenate([x[n * count : (n + 1) * count] for n in range(4)], axis=1)
        stacked = layer_norm(x).astype(BF16)
        merge_w.wait()
        merged = jnp.dot(stacked[:, :here], first_ref[...], preferred_element_type=F32)
        merged = merged + jnp.dot(stacked[:, here:], merge_ref[...], preferred_element_type=F32)
        merged = merged.astype(BF16).astype(F32)
        normed = layer_norm(merged).astype(BF16)
        qkv_w.wait()
        proj_w.wait()
        qkv_ref[...] = jnp.dot(normed, qkv_w_ref[...], preferred_element_type=F32).astype(BF16)

        def finish(w, out):
            out = jnp.dot(out, proj_w_ref[...], preferred_element_type=F32)
            out_ref[...] = (merged + out).astype(BF16)

        attend_windows(lambda w, at: qkv_ref[:, at : at + 128], lambda w: id_ref[...], 1, inner, finish)
        sent = select_rows(columns_of(rows_of(plan, rows_ref, "send_three"), sum(plan.room_three)), out_ref[...])
        sent = sent.astype(BF16)
        for n, sizes in enumerate(plan.three):

            @pl.when(flags_ref[0] == n)
            def _():
                at = 0
                for ref, size, space in zip(piece_outs, sizes, plan.room_three):
                    ref[:size, :] = sent[at : at + size, :half]
                    ref[size : 2 * size, :] = sent[at : at + size, half:]
                    at += space

        for n, fine_sizes in enumerate(plan.four):
            if sum(fine_sizes):

                @pl.when(flags_ref[0] == n)
                def _():
                    at = 0
                    for ref, size, more, space in zip(piece_outs, plan.three[n], fine_sizes, plan.room_four):
                        ref[2 * size : 2 * size + more, :] = home_ref[at : at + more, :]
                        at += space

    most = [max(2 * three[k] + four[k] for three, four in zip(plan.three, plan.four)) for k in range(3)]
    outs = shapes([count], width) + shapes(most, half)
    scratch = [pltpu.VMEM((count, 3 * inner), BF16)]
    shapes_in = [(count, 128), (depth - merge_first.shape[0], width), w_qkv.shape, w_proj.shape]
    scratch += [pltpu.VMEM(shape, BF16) for shape in shapes_in]
    args = [flags, w_merge, w_qkv, w_proj, home, x_own, source, ids, merge_first, rows]
    in_specs = [SMEM] + [HBM] * 3 + [VMEM] * (len(args) - 4)
    out, *sent = call(body, outs, args, in_specs, scratch, 3, 3 << 30, 12 << 20, 24)
    return out, sent


def fine_output(part, source, rows, plan, block_rows, block_cols, partial):
    own, width = part.shape

    def body(part_hbm, source_ref, rows_ref, out_ref, part_ref, stage_ref, sems):
        start = Copies(sems)
        cuts = [pl.ds(at, TOK) for at in range(0, own, TOK)]
        held = [start(part_hbm.at[cut], part_ref.at[cut]) for cut in cuts]
        take = columns_of(rows_of(plan, rows_ref, "fine_out"), own) - float(own)
        leave = []
        for n, (cut, copy) in enumerate(zip(cuts, held)):
            got = select_rows(take[n * TOK : (n + 1) * TOK], source_ref[...])
            copy.wait()
            out = part_ref[cut, :].astype(F32) + got
            if partial:
                out_ref[cut, :] = out.astype(BF16)
            else:
                lines = TOK // block_cols
                layer, line = divmod(n * lines, block_rows)
                there = (layer, pl.ds(line, lines))
                stage_ref[there] = out.reshape(lines, block_cols, width).astype(BF16)
                leave.append(start(stage_ref.at[there], out_ref.at[there]))
        for copy in leave:
            copy.wait()

    shape = (2, block_rows, block_cols, width)
    outs = shapes([own], width) if partial else [pltpu.HBM(shape, BF16)]
    scratch = [pltpu.VMEM(part.shape, BF16), pltpu.VMEM(shape, BF16)]
    return call(body, outs, [part, source, rows], [HBM, VMEM, VMEM], scratch, 2 * own // TOK, 1 << 30, 4 << 20)[0]


def coarse_output(coarse, got, rows, which, plan, block_rows, block_cols, part=None):
    own, width = coarse.shape
    half = width // 2
    sizes, more = plan.three[which], plan.four[which]
    parts = [] if part is None else [part]

    def padded(parts, sizes, room):
        out = []
        for value, size, space in zip(parts, sizes, room):
            out.append(value)
            if size < space:
                out.append(jnp.zeros((space - size, value.shape[1]), F32))
        return out

    def body(coarse_ref, *refs):
        got_refs, refs = refs[:3], refs[3:]
        part_refs, (rows_ref, out_ref, *fine_outs, _) = refs[: len(parts)], refs[len(parts) :]
        got = [ref[...].astype(F32) for ref in got_refs]
        back = [jnp.concatenate([x[:size], x[size : 2 * size]], axis=1) for x, size in zip(got, sizes)]
        source = stack_rows([coarse_ref[...].astype(F32)] + padded(back, sizes, plan.room_three))
        out = select_rows(columns_of(rows_of(plan, rows_ref, "coarse_out"), own), source.astype(BF16)).astype(BF16)
        for n in range(own // 2):
            out_ref[n // block_cols, n % block_cols] = out[2 * n : 2 * n + 2]
        for part_ref, fine_ref in zip(part_refs, fine_outs):
            fine = stack_rows(padded([x[2 * size :] for x, size in zip(got, sizes)], more, plan.room_four))
            base = part_ref.shape[0] + sum(plan.room_two)
            take = columns_of(rows_of(plan, rows_ref, "fine_out"), part_ref.shape[0]) - float(base)
            out = part_ref[...].astype(F32) + select_rows(take, fine.astype(BF16))
            fine_ref[...] = out.reshape(fine_ref.shape).astype(BF16)

    outs = [jax.ShapeDtypeStruct((block_rows, block_cols, 2, width), BF16)]
    outs += [jax.ShapeDtypeStruct((2, 2 * block_rows, 2 * block_cols, half), BF16) for _ in parts]
    args = [coarse, *got, *parts, rows]
    out, *fine = call(body, outs, args, [VMEM] * len(args), [], 1, 1 << 28, 1 << 20)
    return out.transpose(2, 0, 1, 3), *fine


def on_device(tokens, regions, shifts, fine_qkv, fine_proj, merge_weight, coarse_qkv, coarse_proj):
    _, rows, cols, _ = tokens.shape
    plan = Plan(rows, cols)

    def first(which, sign, sent, *args):
        got = exchange(sent, plan.one[which], sign)
        return lay(got, plan.room_one), before_fine(*args, plan, rows, cols)

    def second(which, sign, sent, *args):
        got = lay(exchange(sent, plan.two[which], sign), plan.room_two)
        if got is None:
            got = zeros((sum(plan.room_two), sent[0].shape[1]))
        return got, before_coarse(*args, plan)

    def third(which, sign, sent, part, source, coarse, table):
        sizes = [2 * n + m for n, m in zip(plan.three[which], plan.four[which])]
        got = exchange(sent, sizes, sign)
        partial = sum(plan.four[which]) > 0
        fine_out = fine_output(part, source, table, plan, rows, cols, partial)
        place = (table, which, plan, rows // 2, cols // 2)
        if partial:
            coarse_out, fine_out = coarse_output(coarse, got, *place, part=fine_out)
        else:
            (coarse_out,) = coarse_output(coarse, got, *place)
        return fine_out, coarse_out

    def branches(stage, pairs):
        return [functools.partial(stage, which, sign) for which, sign in pairs]

    sent, source, table, flags, one, two, three = first_pieces(shifts, tokens, plan)
    got, (ids, x, weights) = choose(
        one, branches(first, plan.one_branches), sent, flags, regions, source, table, [fine_qkv, fine_proj]
    )
    fine, sent = fine_level(x, got, ids, *weights, fine_qkv, table, plan)
    got, (x, part, home, merge_first) = choose(
        two, branches(second, plan.two_branches), sent, flags, fine, table, merge_weight
    )
    coarse, sent = coarse_level(
        flags, home, x, got, ids, merge_first, merge_weight, coarse_qkv, coarse_proj, table, plan
    )
    return choose(three, branches(third, plan.three_branches), sent, part, got, coarse, table)


def solution(mesh):
    return jax.shard_map(
        on_device,
        mesh=mesh,
        in_specs=(P(None, "lat", "lon", None), P(), P(), P(), P(), P(), P(), P()),
        out_specs=(P(None, "lat", "lon", None), P(None, "lat", "lon", None)),
        check_vma=False,
    )
```

profile of v0, /device:TPU:0, one launch (start us, length us, event | category | flops | bytes accessed | tf_op | source)
XLA Modules:
  0.0 41.1 jit_solution(2310552382373375592)
XLA Ops:
  0.6 1.6 %shard_map.118 = (bf16[112,512]{1,0:T(8,128)(2,1)S(1)}, bf16[112,512]{1,0:T(8,128)(2,1)S(1)}, bf16[48,512]{1,0:T(8,128)(2,1)S(1)}, bf16[576,512]{1,0:T(8,128)(2,...) custom-call(s32[2]{0:T(128)} %shifts_hbm.1, ...), custom_call_target="tpu_custom_call" | custom-call | flops 268435456 | bytes 1048576 | tf_op jit(solution)/shard_map/pallas_call | solution.py:275
  2.2 11.6 %conditional.3 = (bf16[272,512]{1,0:T(8,128)(2,1)S(1)}, f32[7,128]{1,0:T(8,128)S(1)}, bf16[576,512]{1,0:T(8,128)(2,1)S(1)}, bf16[512,1024]{1,0:T(8,128)(2,1)S(1)}, bf16[512,512]{1,0:T(8,128)(2,1)S(1)}) conditional(s32[]{:T(128)S(4)} %bitcast.14, (bf16[112,512]{1,0:T(8,128)(2,1)S(1)}, bf16[112,512]{1,0:T(8,128)(2,1)S(1)}, ...), branch_computations={%region_0.0_spmd, %region_1.0_spmd, %region_2.0_spmd, %region_3.0_... | conditional | flops 268435456 | bytes 5619872 | solution.py:368
  2.3 0.5 %collective-permute-start.12 = (bf16[112,512]{1,0:T(8,128)(2,1)S(1)}, bf16[112,512]{1,0:T(8,128)(2,1)S(1)}, u32[]{:S(2)}, u32[]{:S(2)}) collective-permute-start(bf16[112,512]{1,0:T(8,128)(2,1)S(1)} %get-tuple-element.332), channel_id=1, source_target_pairs={{28,0},{0,4},{4,8},{8,12},{12,16},{16,20},{20,24},{24,28},{29,1},{... | collective-permute-start | bytes 344072 | tf_op jit(solution)/shard_map/cond/branch_4_fun/ppermute | solution.py:352
  2.8 2.6 %collective-permute-start.13 = (bf16[112,512]{1,0:T(8,128)(2,1)S(1)}, bf16[112,512]{1,0:T(8,128)(2,1)S(1)}, u32[]{:S(2)}, u32[]{:S(2)}) collective-permute-start(bf16[112,512]{1,0:T(8,128)(2,1)S(1)} %get-tuple-element.333), channel_id=1, source_target_pairs={{3,0},{0,1},{1,2},{2,3},{7,4},{4,5},{5,6},{6,7},{11,8},{8,9},{9,10... | collective-permute-start | bytes 344072 | tf_op jit(solution)/shard_map/cond/branch_4_fun/ppermute | solution.py:350
  5.4 2.4 %collective-permute-start.14 = (bf16[40,512]{1,0:T(8,128)(2,1)S(1)}, bf16[40,512]{1,0:T(8,128)(2,1)S(1)}, u32[]{:S(2)}, u32[]{:S(2)}) collective-permute-start(bf16[40,512]{1,0:T(8,128)(2,1)S(1)} %slice.98), channel_id=1, source_target_pairs={{31,0},{28,1},{29,2},{30,3},{3,4},{0,5},{1,6},{2,7},{7,8},{4,9},{5... | collective-permute-start | bytes 122888 | tf_op jit(solution)/shard_map/cond/branch_4_fun/ppermute | solution.py:351
  7.8 1.7 %branch_4_fun.7 = (f32[7,128]{1,0:T(8,128)S(1)}, bf16[576,512]{1,0:T(8,128)(2,1)S(1)}, bf16[512,1024]{1,0:T(8,128)(2,1)S(1)}, bf16[512,512]{1,0:T(8,128)(2,1)S(1)}) custom-call(s32[8]{0:T(128)S(4)} %get-tuple-element.335.flags_ref, f32[32,128]{1,0:T(8,128)S(1)} %get-tuple-element.336.rows_ref, bf16[576,512]{1,0:T(8,128)(2,1)S(1)} %get-tuple-element.337.tokens_ref, ...), custom_call_target="tpu_custom_call" | custom-call | flops 268435456 | bytes 4194304 | tf_op jit(solution)/shard_map/cond/branch_4_fun/pallas_call | solution.py:275
  9.6 4.2 %collective-permute-done.14.refs_2_ = bf16[40,512]{1,0:T(8,128)(2,1)S(1)} collective-permute-done((bf16[40,512]{1,0:T(8,128)(2,1)S(1)}, bf16[40,512]{1,0:T(8,128)(2,1)S(1)}, u32[]{:S(2)}, u32[]{:S(2)}) %collective-permute-start.14) | collective-permute-done | bytes 40992 | tf_op jit(solution)/shard_map/cond/branch_4_fun/ppermute | solution.py:351
  13.7 0.0 collective-permute-done.12.refs_0_
  13.7 0.0 collective-permute-done.13.refs_1_
  13.8 5.9 %shard_map.119 = (bf16[576,512]{1,0:T(8,128)(2,1)S(1)}, bf16[160,512]{1,0:T(8,128)(2,1)S(1)}, bf16[160,512]{1,0:T(8,128)(2,1)S(1)}, bf16[112,512]{1,0:T(8,128)(2,1)S(1)}) custom-call(bf16[576,512]{1,0:T(8,128)(2,1)S(1)} %get-tuple-element.514.own_ref, bf16[272,512]{1,0:T(8,128)(2,1)S(1)} %get-tuple-element.515.source_ref, ...), custom_call_target="tpu_custom_call" | custom-call | flops 3221225472 | bytes 6291456 | tf_op jit(solution)/shard_map/pallas_call | solution.py:275
  19.6 5.9 %conditional.4 = (bf16[432,512]{1,0:T(8,128)(2,1)S(1)}, bf16[576,512]{1,0:T(8,128)(2,1)S(1)}, bf16[576,512]{1,0:T(8,128)(2,1)}, bf16[176,512]{1,0:T(8,128)(2,1)S(1)}, bf16[576,1024]{1,0:T(8,128)(2,1)S(1)}) conditional(s32[]{:T(128)S(4)} %bitcast.13, (s32[8]{0:T(128)S(4)}, f32[32,128]{1,0:T(8,128)S(1)}, ...), branch_computations={%region_5.0_spmd, %region_6.0_spmd, %region_7.0_spmd, %region_8.0_... | conditional | flops 268435456 | bytes 6619296 | solution.py:368
  19.9 1.7 %collective-permute-start.22 = (bf16[120,512]{1,0:T(8,128)(2,1)S(1)}, bf16[120,512]{1,0:T(8,128)(2,1)S(1)}, u32[]{:S(2)}, u32[]{:S(2)}) collective-permute-start(bf16[120,512]{1,0:T(8,128)(2,1)S(1)} %slice.106), channel_id=1, source_target_pairs={{1,0},{2,1},{3,2},{0,3},{5,4},{6,5},{7,6},{4,7},{9,8},{10,9},{11,1... | collective-permute-start | bytes 368648 | tf_op jit(solution)/shard_map/cond/branch_3_fun/ppermute | solution.py:350
  21.6 0.4 %collective-permute-start.21 = (bf16[120,512]{1,0:T(8,128)(2,1)S(1)}, bf16[120,512]{1,0:T(8,128)(2,1)S(1)}, u32[]{:S(2)}, u32[]{:S(2)}) collective-permute-start(bf16[120,512]{1,0:T(8,128)(2,1)S(1)} %slice.105), channel_id=1, source_target_pairs={{4,0},{8,4},{12,8},{16,12},{20,16},{24,20},{28,24},{0,28},{5,1},{9... | collective-permute-start | bytes 368648 | tf_op jit(solution)/shard_map/cond/branch_3_fun/ppermute | solution.py:352
  22.0 0.9 %collective-permute-start.23 = (bf16[40,512]{1,0:T(8,128)(2,1)S(1)}, bf16[40,512]{1,0:T(8,128)(2,1)S(1)}, u32[]{:S(2)}, u32[]{:S(2)}) collective-permute-start(bf16[40,512]{1,0:T(8,128)(2,1)S(1)} %slice.107), channel_id=1, source_target_pairs={{5,0},{6,1},{7,2},{4,3},{9,4},{10,5},{11,6},{8,7},{13,8},{14,9},{1... | collective-permute-start | bytes 122888 | tf_op jit(solution)/shard_map/cond/branch_3_fun/ppermute | solution.py:351
  22.9 1.5 %branch_3_fun.9 = (bf16[576,512]{1,0:T(8,128)(2,1)S(1)}, bf16[576,512]{1,0:T(8,128)(2,1)}, bf16[176,512]{1,0:T(8,128)(2,1)S(1)}, bf16[576,1024]{1,0:T(8,128)(2,1)S(1)}) custom-call(s32[8]{0:T(128)S(4)} %get-tuple-element.378.flags_ref, f32[32,128]{1,0:T(8,128)S(1)} %get-tuple-element.379.rows_ref, bf16[576,512]{1,0:T(8,128)(2,1)S(1)} %get-tuple-element.380.fine_ref, ...), custom_call_target="tpu_custom_call" | custom-call | flops 268435456 | bytes 4194304 | tf_op jit(solution)/shard_map/cond/branch_3_fun/pallas_call | solution.py:275
  24.5 1.0 %collective-permute-done.23.refs_2_ = bf16[40,512]{1,0:T(8,128)(2,1)S(1)} collective-permute-done((bf16[40,512]{1,0:T(8,128)(2,1)S(1)}, bf16[40,512]{1,0:T(8,128)(2,1)S(1)}, u32[]{:S(2)}, u32[]{:S(2)}) %collective-permute-start.23) | collective-permute-done | bytes 40992 | tf_op jit(solution)/shard_map/cond/branch_3_fun/ppermute | solution.py:351
  25.5 0.0 collective-permute-done.22.refs_1_
  25.5 0.0 collective-permute-done.21.refs_0_
  25.5 5.0 %shard_map.120 = (bf16[144,1024]{1,0:T(8,128)(2,1)S(1)}, bf16[128,512]{1,0:T(8,128)(2,1)S(1)}, bf16[128,512]{1,0:T(8,128)(2,1)S(1)}, bf16[88,512]{1,0:T(8,128)(2,1)S(1)}) custom-call(s32[8]{0:T(128)S(4)} %get-tuple-element.507.flags_ref, bf16[2048,1024]{1,0:T(8,128)(2,1)} %merge_hbm.1, bf16[1024,1536]{1,0:T(8,128)(2,1)} %qkv_w_hbm.3, ...), custom_call_target="tpu_custom_call" | custom-call | flops 3221225472 | bytes 12582912 | tf_op jit(solution)/shard_map/pallas_call | solution.py:275
  30.5 10.4 %conditional.5 = (bf16[2,12,24,512]{3,2,1,0:T(8,128)(2,1)}, bf16[2,6,12,1024]{3,0,2,1:T(2,128)(2,1)}) conditional(s32[]{:T(128)S(4)} %bitcast.12, (bf16[576,512]{1,0:T(8,128)(2,1)}, bf16[432,512]{1,0:T(8,128)(2,1)S(1)}, f32[32,128]{1,0:T(8,128)S(1)}, bf16[128,512]{1,0:T(8,128)(2,1)S(1)}, ...), branch_computations={%region_12.0_spmd, %region_13.0_spmd, %region_14.0_spmd, %region_1... | conditional | flops 1342177280 | bytes 6865032 | solution.py:368
  30.5 5.0 %collective-permute-start.38 = (bf16[16,512]{1,0:T(8,128)(2,1)S(1)}, bf16[16,512]{1,0:T(8,128)(2,1)S(1)}, u32[]{:S(2)}, u32[]{:S(2)}) collective-permute-start(bf16[16,512]{1,0:T(8,128)(2,1)S(1)} %slice.118), channel_id=1, source_target_pairs={{5,0},{6,1},{7,2},{4,3},{9,4},{10,5},{11,6},{8,7},{13,8},{14,9},{1... | collective-permute-start | bytes 49160 | tf_op jit(solution)/shard_map/cond/branch_1_fun/ppermute | solution.py:351
  35.5 0.0 collective-permute-start.37
  35.5 0.4 collective-permute-start.36
  35.9 2.5 %branch_1_fun.10 = bf16[2,12,24,512]{3,2,1,0:T(8,128)(2,1)} custom-call(bf16[576,512]{1,0:T(8,128)(2,1)} %get-tuple-element.426.part_hbm, bf16[432,512]{1,0:T(8,128)(2,1)S(1)} %get-tuple-element.427.source_ref, f32[32,128]{1,0:T(8,128)S(1)} %get-tuple-element.428.rows_ref.refs_3_), custom_call_target="tpu_custom_call" | custom-call | flops 1073741824 | bytes 4194304 | tf_op jit(solution)/shard_map/cond/branch_1_fun/pallas_call | solution.py:275
  38.3 0.0 collective-permute-done.38.refs_2_
  38.4 1.2 %collective-permute-done.37.refs_1_ = bf16[48,512]{1,0:T(8,128)(2,1)S(1)} collective-permute-done((bf16[48,512]{1,0:T(8,128)(2,1)S(1)}, bf16[48,512]{1,0:T(8,128)(2,1)S(1)}, u32[]{:S(2)}, u32[]{:S(2)}) %collective-permute-start.37) | collective-permute-done | bytes 49184 | tf_op jit(solution)/shard_map/cond/branch_1_fun/ppermute | solution.py:350
  39.6 0.0 collective-permute-done.36.refs_0_
  39.6 1.1 %branch_1_fun.11 = bf16[6,12,2,1024]{3,2,1,0:T(2,128)(2,1)} custom-call(bf16[144,1024]{1,0:T(8,128)(2,1)S(1)} %get-tuple-element.429.coarse_ref, bf16[48,512]{1,0:T(8,128)(2,1)S(1)} %collective-permute-done.36.refs_0_, bf16[48,512]{1,0:T(8,128)(2,1)S(1)} %collective-permute-done.37.refs_1_, bf16[16,512]{1,0:T(8,128)(2,1)S(1)} %collective-permute-done.38.refs_2_, ...), custom_call_target="tpu_custom_call" | custom-call | flops 268435456 | bytes 1048576 | tf_op jit(solution)/shard_map/cond/branch_1_fun/pallas_call | solution.py:275
  (9 shorter events, 0.1 us)
Async XLA Ops:
  2.3 11.5 %collective-permute-start.12 = (bf16[112,512]{1,0:T(8,128)(2,1)S(1)}, bf16[112,512]{1,0:T(8,128)(2,1)S(1)}, u32[]{:S(2)}, u32[]{:S(2)}) collective-permute-start(bf16[112,512]{1,0:T(8,128)(2,1)S(1)} %get-tuple-element.332), channel_id=1, source_target_pairs={{28,0},{0,4},{4,8},{8,12},{12,16},{16,20},{20,24},{24,28},{29,1},{... | collective-permute-start | bytes 344072 | tf_op jit(solution)/shard_map/cond/branch_4_fun/ppermute | solution.py:352
  2.8 11.0 %collective-permute-start.13 = (bf16[112,512]{1,0:T(8,128)(2,1)S(1)}, bf16[112,512]{1,0:T(8,128)(2,1)S(1)}, u32[]{:S(2)}, u32[]{:S(2)}) collective-permute-start(bf16[112,512]{1,0:T(8,128)(2,1)S(1)} %get-tuple-element.333), channel_id=1, source_target_pairs={{3,0},{0,1},{1,2},{2,3},{7,4},{4,5},{5,6},{6,7},{11,8},{8,9},{9,10... | collective-permute-start | bytes 344072 | tf_op jit(solution)/shard_map/cond/branch_4_fun/ppermute | solution.py:350
  5.4 8.3 %collective-permute-start.14 = (bf16[40,512]{1,0:T(8,128)(2,1)S(1)}, bf16[40,512]{1,0:T(8,128)(2,1)S(1)}, u32[]{:S(2)}, u32[]{:S(2)}) collective-permute-start(bf16[40,512]{1,0:T(8,128)(2,1)S(1)} %slice.98), channel_id=1, source_target_pairs={{31,0},{28,1},{29,2},{30,3},{3,4},{0,5},{1,6},{2,7},{7,8},{4,9},{5... | collective-permute-start | bytes 122888 | tf_op jit(solution)/shard_map/cond/branch_4_fun/ppermute | solution.py:351
  19.9 5.6 %collective-permute-start.22 = (bf16[120,512]{1,0:T(8,128)(2,1)S(1)}, bf16[120,512]{1,0:T(8,128)(2,1)S(1)}, u32[]{:S(2)}, u32[]{:S(2)}) collective-permute-start(bf16[120,512]{1,0:T(8,128)(2,1)S(1)} %slice.106), channel_id=1, source_target_pairs={{1,0},{2,1},{3,2},{0,3},{5,4},{6,5},{7,6},{4,7},{9,8},{10,9},{11,1... | collective-permute-start | bytes 368648 | tf_op jit(solution)/shard_map/cond/branch_3_fun/ppermute | solution.py:350
  21.6 3.9 %collective-permute-start.21 = (bf16[120,512]{1,0:T(8,128)(2,1)S(1)}, bf16[120,512]{1,0:T(8,128)(2,1)S(1)}, u32[]{:S(2)}, u32[]{:S(2)}) collective-permute-start(bf16[120,512]{1,0:T(8,128)(2,1)S(1)} %slice.105), channel_id=1, source_target_pairs={{4,0},{8,4},{12,8},{16,12},{20,16},{24,20},{28,24},{0,28},{5,1},{9... | collective-permute-start | bytes 368648 | tf_op jit(solution)/shard_map/cond/branch_3_fun/ppermute | solution.py:352
  22.0 3.4 %collective-permute-start.23 = (bf16[40,512]{1,0:T(8,128)(2,1)S(1)}, bf16[40,512]{1,0:T(8,128)(2,1)S(1)}, u32[]{:S(2)}, u32[]{:S(2)}) collective-permute-start(bf16[40,512]{1,0:T(8,128)(2,1)S(1)} %slice.107), channel_id=1, source_target_pairs={{5,0},{6,1},{7,2},{4,3},{9,4},{10,5},{11,6},{8,7},{13,8},{14,9},{1... | collective-permute-start | bytes 122888 | tf_op jit(solution)/shard_map/cond/branch_3_fun/ppermute | solution.py:351
  30.5 7.8 %collective-permute-start.38 = (bf16[16,512]{1,0:T(8,128)(2,1)S(1)}, bf16[16,512]{1,0:T(8,128)(2,1)S(1)}, u32[]{:S(2)}, u32[]{:S(2)}) collective-permute-start(bf16[16,512]{1,0:T(8,128)(2,1)S(1)} %slice.118), channel_id=1, source_target_pairs={{5,0},{6,1},{7,2},{4,3},{9,4},{10,5},{11,6},{8,7},{13,8},{14,9},{1... | collective-permute-start | bytes 49160 | tf_op jit(solution)/shard_map/cond/branch_1_fun/ppermute | solution.py:351
  35.5 4.1 %collective-permute-start.37 = (bf16[48,512]{1,0:T(8,128)(2,1)S(1)}, bf16[48,512]{1,0:T(8,128)(2,1)S(1)}, u32[]{:S(2)}, u32[]{:S(2)}) collective-permute-start(bf16[48,512]{1,0:T(8,128)(2,1)S(1)} %slice.117), channel_id=1, source_target_pairs={{1,0},{2,1},{3,2},{0,3},{5,4},{6,5},{7,6},{4,7},{9,8},{10,9},{11,1... | collective-permute-start | bytes 147464 | tf_op jit(solution)/shard_map/cond/branch_1_fun/ppermute | solution.py:350
  35.5 4.1 %collective-permute-start.36 = (bf16[48,512]{1,0:T(8,128)(2,1)S(1)}, bf16[48,512]{1,0:T(8,128)(2,1)S(1)}, u32[]{:S(2)}, u32[]{:S(2)}) collective-permute-start(bf16[48,512]{1,0:T(8,128)(2,1)S(1)} %slice.116), channel_id=1, source_target_pairs={{4,0},{8,4},{12,8},{16,12},{20,16},{24,20},{28,24},{0,28},{5,1},{9... | collective-permute-start | bytes 147464 | tf_op jit(solution)/shard_map/cond/branch_1_fun/ppermute | solution.py:352
where the time goes:
time: 40.4 us; the launch traced here: 41.1 us
  Pallas kernels  19.3 us (48%)
  starting transfers between devices  14 us (35%)
  waiting for transfers between devices  6.38 us (16%)
  between operations  0.85 us (2%)
  loops' own time  0.61 us (2%)
    pallas_call x9, Pallas kernels, call(): pl.pallas_call(body, out_shape=outs, in_specs=in_specs, out_specs=out_spe...  19.3 us
    ppermute x3, starting transfers between devices, exchange(): both = lax.ppermute(both, ('lat', 'lon'), pairs)  8.32 us
    ppermute x3, waiting for transfers between devices, exchange(): both = lax.ppermute(both, ('lat', 'lon'), pairs)  5.13 us
    ppermute x3, starting transfers between devices, exchange(): col = lax.ppermute(col, 'lon', [((j + sign) % lon, j) for j in range(lon)])  4.37 us
    ppermute x3, starting transfers between devices, exchange(): row = lax.ppermute(row, 'lat', [((i + sign) % lat, i) for i in range(lat)])  1.28 us
    ppermute x3, waiting for transfers between devices, exchange(): col = lax.ppermute(col, 'lon', [((j + sign) % lon, j) for j in range(lon)])  1.24 us
  transfers between devices with their start and end apart: 9, of which 3 were waited for; matrix products, arithmetic and copies ran while one was open for 0% of the time, Pallas kernels for 14%

commit v1 on v0

--- a/solution.py
+++ b/solution.py
@@ -379,7 +379,7 @@
 
     def body(shifts_hbm, tokens_hbm, table_hbm, *refs):
         outs, refs = refs[:kinds], refs[kinds:]
-        source_ref, rows_ref, flags_ref, *at_refs, shifts_ref, tokens_ref, table_ref, sems = refs
+        rows_ref, flags_ref, *at_refs, shifts_ref, tokens_ref, table_ref, source_ref, sems = refs
         start = Copies(sems)
         shift = start(shifts_hbm, shifts_ref)
         held = start(tokens_hbm, tokens_ref)
@@ -397,18 +397,19 @@
         index = columns_of(rows_of(plan, table_ref, "send_one", case), sum(plan.room_one))
         put_pieces(select_rows(index, source_ref[...]), outs)
 
-    outs = shapes([*plan.room_one, count], width)
+    outs = shapes(plan.room_one, width)
     outs += [pltpu.VMEM(plan.table.shape[1:], F32), pltpu.SMEM((8,), I32)]
     outs += [pltpu.SMEM((1,), I32)] * 3
     scratch = [pltpu.SMEM((2,), I32), pltpu.VMEM(tokens.shape, BF16), pltpu.VMEM(plan.table.shape, F32)]
+    scratch += [pltpu.VMEM((count, width), BF16)]
     got = call(body, outs, [shifts, tokens, plan.table], [HBM] * 3, scratch, 3, 1 << 28, 1 << 20)
-    sent, (source, rows, flags, one, two, three) = got[:kinds], got[kinds:]
-    return sent, source, rows, flags, one[0], two[0], three[0]
-
-
-def before_fine(flags, regions, tokens, table, weights, plan, rows, cols):
+    sent, (rows, flags, one, two, three) = got[:kinds], got[kinds:]
+    return sent, rows, flags, one[0], two[0], three[0]
+
+
+def before_fine(flags, regions, tokens, table, weights, plan):
     _, lat, lon = regions.shape
-    width = tokens.shape[1]
+    _, rows, cols, width = tokens.shape
     flat_regions = regions.reshape(2 * lat, lon)
     fine, coarse = windowed(rows, cols), natural(rows // 2, cols // 2)
 
@@ -419,15 +420,14 @@
     places = np.concatenate([lanes(fine, 1, 1), lanes(coarse, 2, 0)], axis=1)
     lines = places.shape[1]
 
-    def body(flags_ref, rows_ref, tokens_ref, regions_hbm, places_hbm, *refs):
+    def body(flags_ref, rows_ref, tokens_hbm, regions_hbm, places_hbm, *refs):
         weights_hbm, refs = refs[: len(weights)], refs[len(weights) :]
         id_ref, x_ref, *refs = refs
-        weight_refs, (regions_ref, places_ref, sems) = refs[: len(weights)], refs[len(weights) :]
+        weight_refs, (regions_ref, places_ref, tokens_ref, sems) = refs[: len(weights)], refs[len(weights) :]
         start = Copies(sems)
         waits = [start(regions_hbm, regions_ref), start(places_hbm, places_ref)]
-        later = [
-            start(src.at[:, pl.ds(0, dst.shape[1])], dst) for src, dst in zip(weights_hbm, weight_refs)
-        ]
+        held = start(tokens_hbm, tokens_ref)
+        later = [start(src, dst) for src, dst in zip(weights_hbm, weight_refs)]
         for copy in waits:
             copy.wait()
         a = flags_ref[1].astype(F32)
@@ -453,16 +453,17 @@
         for n in range(lines):
             id_ref[n : n + 1, :] = ids[:, n * 128 : (n + 1) * 128]
         take = columns_of(rows_of(plan, rows_ref, "take_one"), len(fine))
-        x_ref[...] = select_rows(take, tokens_ref[...]).astype(BF16)
+        held.wait()
+        x_ref[...] = select_rows(take, flat(tokens_ref)).astype(BF16)
         for copy in later:
             copy.wait()
 
     outs = [pltpu.VMEM((lines, 128), F32)] + shapes([len(fine)], width)
-    outs += [pltpu.VMEM((w.shape[0], min(w.shape[1], 2 * weights[1].shape[0])), BF16) for w in weights]
-    scratch = [pltpu.VMEM(flat_regions.shape, I32), pltpu.VMEM(places.shape, F32)]
+    outs += [pltpu.VMEM(w.shape, BF16) for w in weights]
+    scratch = [pltpu.VMEM(flat_regions.shape, I32), pltpu.VMEM(places.shape, F32), pltpu.VMEM(tokens.shape, BF16)]
     args = [flags, table, tokens, flat_regions, places, *weights]
-    in_specs = [SMEM, VMEM, VMEM] + [HBM] * (2 + len(weights))
-    ids, x, *weights = call(body, outs, args, in_specs, scratch, 2 + len(weights), 1 << 28, 4 << 20)
+    in_specs = [SMEM, VMEM] + [HBM] * (3 + len(weights))
+    ids, x, *weights = call(body, outs, args, in_specs, scratch, 3 + len(weights), 1 << 28, 4 << 20)
     return ids, x, weights
 
 
@@ -504,21 +505,18 @@
     return functools.reduce(jnp.logical_or, [flags_ref[0] == n for n in with_fine])
 
 
-def fine_level(x_own, source, ids, w_qk, w_proj, w_qkv, rows, plan):
+def fine_level(x_own, source, ids, w_qkv, w_proj, rows, plan):
     count, width = x_own.shape
     inner = w_proj.shape[0]
 
-    def body(own_ref, source_ref, ids_ref, qk_w_ref, proj_w_ref, qkv_w_hbm, rows_ref, out_ref, *refs):
-        *piece_outs, x_ref, qkv_ref, id_ref, v_w_ref, sems = refs
-        v_w = Copies(sems)(qkv_w_hbm.at[:, pl.ds(2 * inner, inner)], v_w_ref)
+    def body(own_ref, source_ref, ids_ref, qkv_w_ref, proj_w_ref, rows_ref, out_ref, *refs):
+        *piece_outs, x_ref, qkv_ref, id_ref, _ = refs
         id_ref[...] = id_columns(ids_ref[: -(-count // 128), :], count)
         take = columns_of(rows_of(plan, rows_ref, "take_one"), count) - float(count)
         x = own_ref[...].astype(F32) + select_rows(take, source_ref[...])
         x_ref[...] = x
         normed = layer_norm(x).astype(BF16)
-        v_w.wait()
-        qkv_ref[:, : 2 * inner] = jnp.dot(normed, qk_w_ref[...], preferred_element_type=F32).astype(BF16)
-        qkv_ref[:, 2 * inner :] = jnp.dot(normed, v_w_ref[...], preferred_element_type=F32).astype(BF16)
+        qkv_ref[...] = jnp.dot(normed, qkv_w_ref[...], preferred_element_type=F32).astype(BF16)
 
         def finish(w, out):
             at = slice(w * TOK, (w + 1) * TOK)
@@ -540,10 +538,9 @@
         pltpu.VMEM((count, width), F32),
         pltpu.VMEM((count, 3 * inner), BF16),
         pltpu.VMEM((count, 128), BF16),
-        pltpu.VMEM((width, inner), BF16),
     ]
-    args = [x_own, source, ids, w_qk, w_proj, w_qkv, rows]
-    out, *sent = call(body, outs, args, [VMEM] * 5 + [HBM, VMEM], scratch, 1, 3 << 30, 6 << 20, 14)
+    args = [x_own, source, ids, w_qkv, w_proj, rows]
+    out, *sent = call(body, outs, args, [VMEM] * len(args), scratch, 1, 3 << 30, 6 << 20, 14)
     return out, sent
 
 
@@ -688,7 +685,7 @@
 
     def first(which, sign, sent, *args):
         got = exchange(sent, plan.one[which], sign)
-        return lay(got, plan.room_one), before_fine(*args, plan, rows, cols)
+        return lay(got, plan.room_one), before_fine(*args, plan)
 
     def second(which, sign, sent, *args):
         got = lay(exchange(sent, plan.two[which], sign), plan.room_two)
@@ -711,11 +708,11 @@
     def branches(stage, pairs):
         return [functools.partial(stage, which, sign) for which, sign in pairs]
 
-    sent, source, table, flags, one, two, three = first_pieces(shifts, tokens, plan)
+    sent, table, flags, one, two, three = first_pieces(shifts, tokens, plan)
     got, (ids, x, weights) = choose(
-        one, branches(first, plan.one_branches), sent, flags, regions, source, table, [fine_qkv, fine_proj]
+        one, branches(first, plan.one_branches), sent, flags, regions, tokens, table, [fine_qkv, fine_proj]
     )
-    fine, sent = fine_level(x, got, ids, *weights, fine_qkv, table, plan)
+    fine, sent = fine_level(x, got, ids, *weights, table, plan)
     got, (x, part, home, merge_first) = choose(
         two, branches(second, plan.two_branches), sent, flags, fine, table, merge_weight
     )

time: 40.4 us -> 41.2 us (1.020)
  local copies, waits for them, and re-layouts: 0.04 us -> 1.86 us
  waiting for transfers between devices: 6.38 us -> 5.46 us
    unnamed x0 -> x2, local copies, waits for them, and re-layouts: none -> 1.04 us
    ppermute x3, waiting for transfers between devices: 5.13 us -> 4.22 us  [exchange(): both = lax.ppermute(both, ('lat', 'lon'), pairs)]
    cond x0 -> x2, local copies, waits for them, and re-layouts: none -> 0.79 us
where the time goes in v1:
time: 41.2 us; the launch traced here: 42 us
  Pallas kernels  19.2 us (47%)
  starting transfers between devices  14 us (34%)
  waiting for transfers between devices  5.46 us (13%)
  local copies, waits for them, and re-layouts  1.86 us (5%)
  between operations  0.86 us (2%)
  loops' own time  0.62 us (2%)
    pallas_call x9, Pallas kernels, call(): pl.pallas_call(body, out_shape=outs, in_specs=in_specs, out_specs=out_spe...  19.2 us
    ppermute x3, starting transfers between devices, exchange(): both = lax.ppermute(both, ('lat', 'lon'), pairs)  8.34 us
    ppermute x3, starting transfers between devices, exchange(): col = lax.ppermute(col, 'lon', [((j + sign) % lon, j) for j in range(lon)])  4.37 us
    ppermute x3, waiting for transfers between devices, exchange(): both = lax.ppermute(both, ('lat', 'lon'), pairs)  4.22 us
    ppermute x3, starting transfers between devices, exchange(): row = lax.ppermute(row, 'lat', [((i + sign) % lat, i) for i in range(lat)])  1.27 us
    ppermute x3, waiting for transfers between devices, exchange(): col = lax.ppermute(col, 'lon', [((j + sign) % lon, j) for j in range(lon)])  1.24 us
    unnamed x2, local copies, waits for them, and re-layouts  1.04 us
  transfers between devices with their start and end apart: 9, of which 3 were waited for; matrix products, arithmetic and copies ran while one was open for 0% of the time, Pallas kernels for 14%

profile of v1, /device:TPU:0, one launch (start us, length us, event | category | flops | bytes accessed | tf_op | source)
XLA Modules:
  0.0 42.0 jit_solution(2060845705182852930)
XLA Ops:
  0.6 1.6 %shard_map.118 = (bf16[112,512]{1,0:T(8,128)(2,1)S(1)}, bf16[112,512]{1,0:T(8,128)(2,1)S(1)}, bf16[48,512]{1,0:T(8,128)(2,1)S(1)}, f32[32,128]{1,0:T(8,128)S(1)}...) custom-call(s32[2]{0:T(128)} %shifts_hbm.1, bf16[2,12,24,512]{3,2,1,0:T(8,128)(2,1)} %tokens_hbm.1, ...), custom_call_target="tpu_custom_call" | custom-call | flops 268435456 | bytes 1048576 | tf_op jit(solution)/shard_map/pallas_call | solution.py:275
  2.2 11.6 %conditional.3 = (bf16[272,512]{1,0:T(8,128)(2,1)S(1)}, f32[7,128]{1,0:T(8,128)S(1)}, bf16[576,512]{1,0:T(8,128)(2,1)S(1)}, bf16[512,1536]{1,0:T(8,128)(2,1)S(1)}, bf16[512,512]{1,0:T(8,128)(2,1)}) conditional(s32[]{:T(128)S(4)} %bitcast.14, (bf16[112,512]{1,0:T(8,128)(2,1)S(1)}, bf16[112,512]{1,0:T(8,128)(2,1)S(1)}, ...), branch_computations={%region_0.0_spmd, %region_1.0_spmd, %region_2.0_spmd, %region_3.0_... | conditional | flops 268435456 | bytes 7717052 | solution.py:368
  2.3 0.5 %collective-permute-start.12 = (bf16[112,512]{1,0:T(8,128)(2,1)S(1)}, bf16[112,512]{1,0:T(8,128)(2,1)S(1)}, u32[]{:S(2)}, u32[]{:S(2)}) collective-permute-start(bf16[112,512]{1,0:T(8,128)(2,1)S(1)} %get-tuple-element.332), channel_id=1, source_target_pairs={{28,0},{0,4},{4,8},{8,12},{12,16},{16,20},{20,24},{24,28},{29,1},{... | collective-permute-start | bytes 344072 | tf_op jit(solution)/shard_map/cond/branch_4_fun/ppermute | solution.py:352
  2.8 2.6 %collective-permute-start.13 = (bf16[112,512]{1,0:T(8,128)(2,1)S(1)}, bf16[112,512]{1,0:T(8,128)(2,1)S(1)}, u32[]{:S(2)}, u32[]{:S(2)}) collective-permute-start(bf16[112,512]{1,0:T(8,128)(2,1)S(1)} %get-tuple-element.333), channel_id=1, source_target_pairs={{3,0},{0,1},{1,2},{2,3},{7,4},{4,5},{5,6},{6,7},{11,8},{8,9},{9,10... | collective-permute-start | bytes 344072 | tf_op jit(solution)/shard_map/cond/branch_4_fun/ppermute | solution.py:350
  5.4 2.4 %collective-permute-start.14 = (bf16[40,512]{1,0:T(8,128)(2,1)S(1)}, bf16[40,512]{1,0:T(8,128)(2,1)S(1)}, u32[]{:S(2)}, u32[]{:S(2)}) collective-permute-start(bf16[40,512]{1,0:T(8,128)(2,1)S(1)} %slice.98), channel_id=1, source_target_pairs={{31,0},{28,1},{29,2},{30,3},{3,4},{0,5},{1,6},{2,7},{7,8},{4,9},{5... | collective-permute-start | bytes 122888 | tf_op jit(solution)/shard_map/cond/branch_4_fun/ppermute | solution.py:351
  7.8 1.8 %branch_4_fun.7 = (f32[7,128]{1,0:T(8,128)S(1)}, bf16[576,512]{1,0:T(8,128)(2,1)S(1)}, bf16[512,1536]{1,0:T(8,128)(2,1)S(1)}, bf16[512,512]{1,0:T(8,128)(2,1)S(1)}) custom-call(s32[8]{0:T(128)S(4)} %get-tuple-element.335.flags_ref, f32[32,128]{1,0:T(8,128)S(1)} %get-tuple-element.336.rows_ref, bf16[2,12,24,512]{3,2,1,0:T(8,128)(2,1)} %get-tuple-element.337.tokens_hbm, ...), custom_call_target="tpu_custom_call" | custom-call | flops 268435456 | bytes 4194304 | tf_op jit(solution)/shard_map/cond/branch_4_fun/pallas_call | solution.py:275
  9.7 0.0 copy-start.4
  9.7 0.8 %copy-done.4 = bf16[512,512]{1,0:T(8,128)(2,1)} copy-done((bf16[512,512]{1,0:T(8,128)(2,1)}, bf16[512,512]{1,0:T(8,128)(2,1)S(1)}, u32[]{:S(2)}) %copy-start.4) | copy-done | bytes 524312 | tf_op jit(solution)/shard_map/cond
  10.5 3.3 %collective-permute-done.14.refs_2_ = bf16[40,512]{1,0:T(8,128)(2,1)S(1)} collective-permute-done((bf16[40,512]{1,0:T(8,128)(2,1)S(1)}, bf16[40,512]{1,0:T(8,128)(2,1)S(1)}, u32[]{:S(2)}, u32[]{:S(2)}) %collective-permute-start.14) | collective-permute-done | bytes 40992 | tf_op jit(solution)/shard_map/cond/branch_4_fun/ppermute | solution.py:351
  13.7 0.0 collective-permute-done.12.refs_0_
  13.7 0.0 collective-permute-done.13.refs_1_
  13.8 0.0 copy-start.5
  13.8 1.0 %copy-done.5 = bf16[512,512]{1,0:T(8,128)(2,1)S(1)} copy-done((bf16[512,512]{1,0:T(8,128)(2,1)S(1)}, bf16[512,512]{1,0:T(8,128)(2,1)}, u32[]{:S(2)}) %copy-start.5) | copy-done | bytes 524312
  14.8 5.6 %shard_map.119 = (bf16[576,512]{1,0:T(8,128)(2,1)S(1)}, bf16[160,512]{1,0:T(8,128)(2,1)S(1)}, bf16[160,512]{1,0:T(8,128)(2,1)S(1)}, bf16[112,512]{1,0:T(8,128)(2,1)S(1)}) custom-call(bf16[576,512]{1,0:T(8,128)(2,1)S(1)} %get-tuple-element.512.own_ref, bf16[272,512]{1,0:T(8,128)(2,1)S(1)} %get-tuple-element.513.source_ref, ...), custom_call_target="tpu_custom_call" | custom-call | flops 3221225472 | bytes 6291456 | tf_op jit(solution)/shard_map/pallas_call | solution.py:275
  20.5 5.9 %conditional.4 = (bf16[432,512]{1,0:T(8,128)(2,1)S(1)}, bf16[576,512]{1,0:T(8,128)(2,1)S(1)}, bf16[576,512]{1,0:T(8,128)(2,1)}, bf16[176,512]{1,0:T(8,128)(2,1)S(1)}, bf16[576,1024]{1,0:T(8,128)(2,1)S(1)}) conditional(s32[]{:T(128)S(4)} %bitcast.13, (s32[8]{0:T(128)S(4)}, f32[32,128]{1,0:T(8,128)S(1)}, ...), branch_computations={%region_5.0_spmd, %region_6.0_spmd, %region_7.0_spmd, %region_8.0_... | conditional | flops 268435456 | bytes 6619296 | solution.py:368
  20.7 1.7 %collective-permute-start.22 = (bf16[120,512]{1,0:T(8,128)(2,1)S(1)}, bf16[120,512]{1,0:T(8,128)(2,1)S(1)}, u32[]{:S(2)}, u32[]{:S(2)}) collective-permute-start(bf16[120,512]{1,0:T(8,128)(2,1)S(1)} %slice.106), channel_id=1, source_target_pairs={{1,0},{2,1},{3,2},{0,3},{5,4},{6,5},{7,6},{4,7},{9,8},{10,9},{11,1... | collective-permute-start | bytes 368648 | tf_op jit(solution)/shard_map/cond/branch_3_fun/ppermute | solution.py:350
  22.4 0.4 collective-permute-start.21
  22.9 0.9 %collective-permute-start.23 = (bf16[40,512]{1,0:T(8,128)(2,1)S(1)}, bf16[40,512]{1,0:T(8,128)(2,1)S(1)}, u32[]{:S(2)}, u32[]{:S(2)}) collective-permute-start(bf16[40,512]{1,0:T(8,128)(2,1)S(1)} %slice.107), channel_id=1, source_target_pairs={{5,0},{6,1},{7,2},{4,3},{9,4},{10,5},{11,6},{8,7},{13,8},{14,9},{1... | collective-permute-start | bytes 122888 | tf_op jit(solution)/shard_map/cond/branch_3_fun/ppermute | solution.py:351
  23.8 1.5 %branch_3_fun.9 = (bf16[576,512]{1,0:T(8,128)(2,1)S(1)}, bf16[576,512]{1,0:T(8,128)(2,1)}, bf16[176,512]{1,0:T(8,128)(2,1)S(1)}, bf16[576,1024]{1,0:T(8,128)(2,1)S(1)}) custom-call(s32[8]{0:T(128)S(4)} %get-tuple-element.378.flags_ref, f32[32,128]{1,0:T(8,128)S(1)} %get-tuple-element.379.rows_ref, bf16[576,512]{1,0:T(8,128)(2,1)S(1)} %get-tuple-element.380.fine_ref, ...), custom_call_target="tpu_custom_call" | custom-call | flops 268435456 | bytes 4194304 | tf_op jit(solution)/shard_map/cond/branch_3_fun/pallas_call | solution.py:275
  25.3 1.0 %collective-permute-done.23.refs_2_ = bf16[40,512]{1,0:T(8,128)(2,1)S(1)} collective-permute-done((bf16[40,512]{1,0:T(8,128)(2,1)S(1)}, bf16[40,512]{1,0:T(8,128)(2,1)S(1)}, u32[]{:S(2)}, u32[]{:S(2)}) %collective-permute-start.23) | collective-permute-done | bytes 40992 | tf_op jit(solution)/shard_map/cond/branch_3_fun/ppermute | solution.py:351
  26.3 0.0 collective-permute-done.22.refs_1_
  26.3 0.0 collective-permute-done.21.refs_0_
  26.4 5.0 %shard_map.120 = (bf16[144,1024]{1,0:T(8,128)(2,1)S(1)}, bf16[128,512]{1,0:T(8,128)(2,1)S(1)}, bf16[128,512]{1,0:T(8,128)(2,1)S(1)}, bf16[88,512]{1,0:T(8,128)(2,1)S(1)}) custom-call(s32[8]{0:T(128)S(4)} %get-tuple-element.506.flags_ref, bf16[2048,1024]{1,0:T(8,128)(2,1)} %merge_hbm.1, bf16[1024,1536]{1,0:T(8,128)(2,1)} %qkv_w_hbm.1, ...), custom_call_target="tpu_custom_call" | custom-call | flops 3221225472 | bytes 12582912 | tf_op jit(solution)/shard_map/pallas_call | solution.py:275
  31.3 10.5 %conditional.5 = (bf16[2,12,24,512]{3,2,1,0:T(8,128)(2,1)}, bf16[2,6,12,1024]{3,0,2,1:T(2,128)(2,1)}) conditional(s32[]{:T(128)S(4)} %bitcast.12, (bf16[576,512]{1,0:T(8,128)(2,1)}, bf16[432,512]{1,0:T(8,128)(2,1)S(1)}, f32[32,128]{1,0:T(8,128)S(1)}, bf16[128,512]{1,0:T(8,128)(2,1)S(1)}, ...), branch_computations={%region_12.0_spmd, %region_13.0_spmd, %region_14.0_spmd, %region_1... | conditional | flops 1342177280 | bytes 6865032 | solution.py:368
  31.4 5.0 %collective-permute-start.38 = (bf16[16,512]{1,0:T(8,128)(2,1)S(1)}, bf16[16,512]{1,0:T(8,128)(2,1)S(1)}, u32[]{:S(2)}, u32[]{:S(2)}) collective-permute-start(bf16[16,512]{1,0:T(8,128)(2,1)S(1)} %slice.118), channel_id=1, source_target_pairs={{5,0},{6,1},{7,2},{4,3},{9,4},{10,5},{11,6},{8,7},{13,8},{14,9},{1... | collective-permute-start | bytes 49160 | tf_op jit(solution)/shard_map/cond/branch_1_fun/ppermute | solution.py:351
  36.3 0.0 collective-permute-start.37
  36.4 0.4 collective-permute-start.36
  36.7 2.5 %branch_1_fun.10 = bf16[2,12,24,512]{3,2,1,0:T(8,128)(2,1)} custom-call(bf16[576,512]{1,0:T(8,128)(2,1)} %get-tuple-element.426.part_hbm, bf16[432,512]{1,0:T(8,128)(2,1)S(1)} %get-tuple-element.427.source_ref, f32[32,128]{1,0:T(8,128)S(1)} %get-tuple-element.428.rows_ref.refs_3_), custom_call_target="tpu_custom_call" | custom-call | flops 1073741824 | bytes 4194304 | tf_op jit(solution)/shard_map/cond/branch_1_fun/pallas_call | solution.py:275
  39.2 0.0 collective-permute-done.38.refs_2_
  39.2 1.2 %collective-permute-done.37.refs_1_ = bf16[48,512]{1,0:T(8,128)(2,1)S(1)} collective-permute-done((bf16[48,512]{1,0:T(8,128)(2,1)S(1)}, bf16[48,512]{1,0:T(8,128)(2,1)S(1)}, u32[]{:S(2)}, u32[]{:S(2)}) %collective-permute-start.37) | collective-permute-done | bytes 49184 | tf_op jit(solution)/shard_map/cond/branch_1_fun/ppermute | solution.py:350
  40.4 0.0 collective-permute-done.36.refs_0_
  40.4 1.1 %branch_1_fun.11 = bf16[6,12,2,1024]{3,2,1,0:T(2,128)(2,1)} custom-call(bf16[144,1024]{1,0:T(8,128)(2,1)S(1)} %get-tuple-element.429.coarse_ref, bf16[48,512]{1,0:T(8,128)(2,1)S(1)} %collective-permute-done.36.refs_0_, bf16[48,512]{1,0:T(8,128)(2,1)S(1)} %collective-permute-done.37.refs_1_, bf16[16,512]{1,0:T(8,128)(2,1)S(1)} %collective-permute-done.38.refs_2_, ...), custom_call_target="tpu_custom_call" | custom-call | flops 268435456 | bytes 1048576 | tf_op jit(solution)/shard_map/cond/branch_1_fun/pallas_call | solution.py:275
  (9 shorter events, 0.1 us)
Async XLA Ops:
  2.3 11.5 %collective-permute-start.12 = (bf16[112,512]{1,0:T(8,128)(2,1)S(1)}, bf16[112,512]{1,0:T(8,128)(2,1)S(1)}, u32[]{:S(2)}, u32[]{:S(2)}) collective-permute-start(bf16[112,512]{1,0:T(8,128)(2,1)S(1)} %get-tuple-element.332), channel_id=1, source_target_pairs={{28,0},{0,4},{4,8},{8,12},{12,16},{16,20},{20,24},{24,28},{29,1},{... | collective-permute-start | bytes 344072 | tf_op jit(solution)/shard_map/cond/branch_4_fun/ppermute | solution.py:352
  2.8 11.0 %collective-permute-start.13 = (bf16[112,512]{1,0:T(8,128)(2,1)S(1)}, bf16[112,512]{1,0:T(8,128)(2,1)S(1)}, u32[]{:S(2)}, u32[]{:S(2)}) collective-permute-start(bf16[112,512]{1,0:T(8,128)(2,1)S(1)} %get-tuple-element.333), channel_id=1, source_target_pairs={{3,0},{0,1},{1,2},{2,3},{7,4},{4,5},{5,6},{6,7},{11,8},{8,9},{9,10... | collective-permute-start | bytes 344072 | tf_op jit(solution)/shard_map/cond/branch_4_fun/ppermute | solution.py:350
  5.4 8.3 %collective-permute-start.14 = (bf16[40,512]{1,0:T(8,128)(2,1)S(1)}, bf16[40,512]{1,0:T(8,128)(2,1)S(1)}, u32[]{:S(2)}, u32[]{:S(2)}) collective-permute-start(bf16[40,512]{1,0:T(8,128)(2,1)S(1)} %slice.98), channel_id=1, source_target_pairs={{31,0},{28,1},{29,2},{30,3},{3,4},{0,5},{1,6},{2,7},{7,8},{4,9},{5... | collective-permute-start | bytes 122888 | tf_op jit(solution)/shard_map/cond/branch_4_fun/ppermute | solution.py:351
  9.7 0.8 %copy-start.4 = (bf16[512,512]{1,0:T(8,128)(2,1)}, bf16[512,512]{1,0:T(8,128)(2,1)S(1)}, u32[]{:S(2)}) copy-start(bf16[512,512]{1,0:T(8,128)(2,1)S(1)} %get-tuple-element.556) | copy-start | bytes 1572868 | tf_op jit(solution)/shard_map/cond
  13.8 1.0 %copy-start.5 = (bf16[512,512]{1,0:T(8,128)(2,1)S(1)}, bf16[512,512]{1,0:T(8,128)(2,1)}, u32[]{:S(2)}) copy-start(bf16[512,512]{1,0:T(8,128)(2,1)} %get-tuple-element.516.proj_w_ref) | copy-start | bytes 1572868
  20.7 5.6 %collective-permute-start.22 = (bf16[120,512]{1,0:T(8,128)(2,1)S(1)}, bf16[120,512]{1,0:T(8,128)(2,1)S(1)}, u32[]{:S(2)}, u32[]{:S(2)}) collective-permute-start(bf16[120,512]{1,0:T(8,128)(2,1)S(1)} %slice.106), channel_id=1, source_target_pairs={{1,0},{2,1},{3,2},{0,3},{5,4},{6,5},{7,6},{4,7},{9,8},{10,9},{11,1... | collective-permute-start | bytes 368648 | tf_op jit(solution)/shard_map/cond/branch_3_fun/ppermute | solution.py:350
  22.4 3.9 %collective-permute-start.21 = (bf16[120,512]{1,0:T(8,128)(2,1)S(1)}, bf16[120,512]{1,0:T(8,128)(2,1)S(1)}, u32[]{:S(2)}, u32[]{:S(2)}) collective-permute-start(bf16[120,512]{1,0:T(8,128)(2,1)S(1)} %slice.105), channel_id=1, source_target_pairs={{4,0},{8,4},{12,8},{16,12},{20,16},{24,20},{28,24},{0,28},{5,1},{9... | collective-permute-start | bytes 368648 | tf_op jit(solution)/shard_map/cond/branch_3_fun/ppermute | solution.py:352
  22.9 3.4 %collective-permute-start.23 = (bf16[40,512]{1,0:T(8,128)(2,1)S(1)}, bf16[40,512]{1,0:T(8,128)(2,1)S(1)}, u32[]{:S(2)}, u32[]{:S(2)}) collective-permute-start(bf16[40,512]{1,0:T(8,128)(2,1)S(1)} %slice.107), channel_id=1, source_target_pairs={{5,0},{6,1},{7,2},{4,3},{9,4},{10,5},{11,6},{8,7},{13,8},{14,9},{1... | collective-permute-start | bytes 122888 | tf_op jit(solution)/shard_map/cond/branch_3_fun/ppermute | solution.py:351
  31.4 7.8 %collective-permute-start.38 = (bf16[16,512]{1,0:T(8,128)(2,1)S(1)}, bf16[16,512]{1,0:T(8,128)(2,1)S(1)}, u32[]{:S(2)}, u32[]{:S(2)}) collective-permute-start(bf16[16,512]{1,0:T(8,128)(2,1)S(1)} %slice.118), channel_id=1, source_target_pairs={{5,0},{6,1},{7,2},{4,3},{9,4},{10,5},{11,6},{8,7},{13,8},{14,9},{1... | collective-permute-start | bytes 49160 | tf_op jit(solution)/shard_map/cond/branch_1_fun/ppermute | solution.py:351
  36.3 4.1 %collective-permute-start.37 = (bf16[48,512]{1,0:T(8,128)(2,1)S(1)}, bf16[48,512]{1,0:T(8,128)(2,1)S(1)}, u32[]{:S(2)}, u32[]{:S(2)}) collective-permute-start(bf16[48,512]{1,0:T(8,128)(2,1)S(1)} %slice.117), channel_id=1, source_target_pairs={{1,0},{2,1},{3,2},{0,3},{5,4},{6,5},{7,6},{4,7},{9,8},{10,9},{11,1... | collective-permute-start | bytes 147464 | tf_op jit(solution)/shard_map/cond/branch_1_fun/ppermute | solution.py:350
  36.4 4.1 %collective-permute-start.36 = (bf16[48,512]{1,0:T(8,128)(2,1)S(1)}, bf16[48,512]{1,0:T(8,128)(2,1)S(1)}, u32[]{:S(2)}, u32[]{:S(2)}) collective-permute-start(bf16[48,512]{1,0:T(8,128)(2,1)S(1)} %slice.116), channel_id=1, source_target_pairs={{4,0},{8,4},{12,8},{16,12},{20,16},{24,20},{28,24},{0,28},{5,1},{9... | collective-permute-start | bytes 147464 | tf_op jit(solution)/shard_map/cond/branch_1_fun/ppermute | solution.py:352

commit v2 on v0

--- a/solution.py
+++ b/solution.py
@@ -118,7 +118,7 @@
             return [[len(numbers) for numbers, _ in case[which]] for case in cases]
 
         self.one, one_class = classes_of(needs(6), 1.15)
-        self.two, two_class = classes_of(needs(7), 1.15)
+        self.two, two_class = classes_of(needs(7), 1.0)
         sizes, three_class = classes_of([three + four for three, four in zip(needs(8), needs(9))], 1.0)
         self.three, self.four = [size[:3] for size in sizes], [size[3:] for size in sizes]
         self.room_one, self.room_two = rooms(self.one), rooms(self.two)

time: 40.4 us -> 39.9 us (0.988); the launches traced: 41.1 us -> 40.2 us
  starting transfers between devices: 14 us -> 11.3 us
  waiting for transfers between devices: 6.38 us -> 8.07 us
    ppermute x3, starting transfers between devices: 8.32 us -> 5.23 us  [exchange(): both = lax.ppermute(both, ('lat', 'lon'), pairs)]
    ppermute x3, waiting for transfers between devices: 5.13 us -> 7.17 us  [exchange(): both = lax.ppermute(both, ('lat', 'lon'), pairs)]
    ppermute x3, starting transfers between devices: 4.37 us -> 4.87 us  [exchange(): col = lax.ppermute(col, 'lon', [((j + sign) % lon, j) for j in range(lon)])]
  transfers between devices with their start and end apart: 9 -> 9, of which waited for: 3 -> 5; matrix products, arithmetic and copies ran while one was open for 0% -> 0% of each run, Pallas kernels for 14% -> 14%
where the time goes in v2:
time: 39.9 us; the launch traced here: 40.2 us
  Pallas kernels  19.3 us (48%)
  starting transfers between devices  11.3 us (28%)
  waiting for transfers between devices  8.07 us (20%)
  between operations  0.87 us (2%)
  loops' own time  0.68 us (2%)
    pallas_call x9, Pallas kernels, call(): pl.pallas_call(body, out_shape=outs, in_specs=in_specs, out_specs=out_spe...  19.3 us
    ppermute x3, waiting for transfers between devices, exchange(): both = lax.ppermute(both, ('lat', 'lon'), pairs)  7.17 us
    ppermute x3, starting transfers between devices, exchange(): both = lax.ppermute(both, ('lat', 'lon'), pairs)  5.23 us
    ppermute x3, starting transfers between devices, exchange(): col = lax.ppermute(col, 'lon', [((j + sign) % lon, j) for j in range(lon)])  4.87 us
    ppermute x3, starting transfers between devices, exchange(): row = lax.ppermute(row, 'lat', [((i + sign) % lat, i) for i in range(lat)])  1.17 us
    ppermute x3, waiting for transfers between devices, exchange(): col = lax.ppermute(col, 'lon', [((j + sign) % lon, j) for j in range(lon)])  0.89 us
  transfers between devices with their start and end apart: 9, of which 5 were waited for; matrix products, arithmetic and copies ran while one was open for 0% of the time, Pallas kernels for 14%

profile of v2, /device:TPU:0, one launch (start us, length us, event | category | flops | bytes accessed | tf_op | source)
XLA Modules:
  0.0 40.2 jit_solution(17124323418781085321)
XLA Ops:
  0.6 1.6 %shard_map.118 = (bf16[112,512]{1,0:T(8,128)(2,1)S(1)}, bf16[112,512]{1,0:T(8,128)(2,1)S(1)}, bf16[48,512]{1,0:T(8,128)(2,1)S(1)}, bf16[576,512]{1,0:T(8,128)(2,...) custom-call(s32[2]{0:T(128)} %shifts_hbm.1, ...), custom_call_target="tpu_custom_call" | custom-call | flops 268435456 | bytes 1048576 | tf_op jit(solution)/shard_map/pallas_call | solution.py:275
  2.2 9.9 %conditional.3 = (bf16[272,512]{1,0:T(8,128)(2,1)S(1)}, f32[7,128]{1,0:T(8,128)S(1)}, bf16[576,512]{1,0:T(8,128)(2,1)S(1)}, bf16[512,1024]{1,0:T(8,128)(2,1)S(1)}, bf16[512,512]{1,0:T(8,128)(2,1)S(1)}) conditional(s32[]{:T(128)S(4)} %bitcast.14, (bf16[112,512]{1,0:T(8,128)(2,1)S(1)}, bf16[112,512]{1,0:T(8,128)(2,1)S(1)}, ...), branch_computations={%region_0.0_spmd, %region_1.0_spmd, %region_2.0_spmd, %region_3.0_... | conditional | flops 268435456 | bytes 5619872 | solution.py:368
  2.2 3.1 %collective-permute-start.1 = (bf16[48,512]{1,0:T(8,128)(2,1)S(1)}, bf16[48,512]{1,0:T(8,128)(2,1)S(1)}, u32[]{:S(2)}, u32[]{:S(2)}) collective-permute-start(bf16[48,512]{1,0:T(8,128)(2,1)S(1)} %slice.97), channel_id=1, source_target_pairs={{3,0},{0,1},{1,2},{2,3},{7,4},{4,5},{5,6},{6,7},{11,8},{8,9},{9,10... | collective-permute-start | bytes 147464 | tf_op jit(solution)/shard_map/cond/branch_0_fun/ppermute | solution.py:350
  5.3 0.0 collective-permute-start
  5.3 2.8 %collective-permute-start.2 = (bf16[8,512]{1,0:T(8,128)(2,1)S(1)}, bf16[8,512]{1,0:T(8,128)(2,1)S(1)}, u32[]{:S(2)}, u32[]{:S(2)}) collective-permute-start(bf16[8,512]{1,0:T(8,128)(2,1)S(1)} %slice.98), channel_id=1, source_target_pairs={{31,0},{28,1},{29,2},{30,3},{3,4},{0,5},{1,6},{2,7},{7,8},{4,9},{5... | collective-permute-start | bytes 24584 | tf_op jit(solution)/shard_map/cond/branch_0_fun/ppermute | solution.py:351
  8.1 1.7 %branch_0_fun.7 = (f32[7,128]{1,0:T(8,128)S(1)}, bf16[576,512]{1,0:T(8,128)(2,1)S(1)}, bf16[512,1024]{1,0:T(8,128)(2,1)S(1)}, bf16[512,512]{1,0:T(8,128)(2,1)S(1)}) custom-call(s32[8]{0:T(128)S(4)} %get-tuple-element.297.flags_ref, f32[32,128]{1,0:T(8,128)S(1)} %get-tuple-element.298.rows_ref, bf16[576,512]{1,0:T(8,128)(2,1)S(1)} %get-tuple-element.299.tokens_ref, ...), custom_call_target="tpu_custom_call" | custom-call | flops 268435456 | bytes 4194304 | tf_op jit(solution)/shard_map/cond/branch_0_fun/pallas_call | solution.py:275
  9.8 2.2 %collective-permute-done.2.refs_2_ = bf16[8,512]{1,0:T(8,128)(2,1)S(1)} collective-permute-done((bf16[8,512]{1,0:T(8,128)(2,1)S(1)}, bf16[8,512]{1,0:T(8,128)(2,1)S(1)}, u32[]{:S(2)}, u32[]{:S(2)}) %collective-permute-start.2) | collective-permute-done | bytes 8224 | tf_op jit(solution)/shard_map/cond/branch_0_fun/ppermute | solution.py:351
  12.1 0.0 collective-permute-done.1.refs_1_
  12.1 0.0 collective-permute-done.refs_0_
  12.1 5.9 %shard_map.119 = (bf16[576,512]{1,0:T(8,128)(2,1)S(1)}, bf16[160,512]{1,0:T(8,128)(2,1)S(1)}, bf16[160,512]{1,0:T(8,128)(2,1)S(1)}, bf16[112,512]{1,0:T(8,128)(2,1)S(1)}) custom-call(bf16[576,512]{1,0:T(8,128)(2,1)S(1)} %get-tuple-element.539.own_ref, bf16[272,512]{1,0:T(8,128)(2,1)S(1)} %get-tuple-element.540.source_ref, ...), custom_call_target="tpu_custom_call" | custom-call | flops 3221225472 | bytes 6291456 | tf_op jit(solution)/shard_map/pallas_call | solution.py:275
  18.0 8.1 %conditional.4 = (bf16[432,512]{1,0:T(8,128)(2,1)S(1)}, bf16[576,512]{1,0:T(8,128)(2,1)S(1)}, bf16[576,512]{1,0:T(8,128)(2,1)}, bf16[176,512]{1,0:T(8,128)(2,1)S(1)}, bf16[576,1024]{1,0:T(8,128)(2,1)S(1)}) conditional(s32[]{:T(128)S(4)} %bitcast.13, (s32[8]{0:T(128)S(4)}, f32[32,128]{1,0:T(8,128)S(1)}, ...), branch_computations={%region_5.0_spmd, %region_6.0_spmd, %region_7.0_spmd, %region_8.0_... | conditional | flops 268435456 | bytes 6865056 | solution.py:368
  18.2 1.2 %collective-permute-start.33 = (bf16[160,512]{1,0:T(8,128)(2,1)S(1)}, bf16[160,512]{1,0:T(8,128)(2,1)S(1)}, u32[]{:S(2)}, u32[]{:S(2)}) collective-permute-start(bf16[160,512]{1,0:T(8,128)(2,1)S(1)} %get-tuple-element.433), channel_id=1, source_target_pairs={{4,0},{8,4},{12,8},{16,12},{20,16},{24,20},{28,24},{0,28},{5,1},{9... | collective-permute-start | bytes 491528 | tf_op jit(solution)/shard_map/cond/branch_7_fun/ppermute | solution.py:352
  19.4 0.5 %collective-permute-start.34 = (bf16[160,512]{1,0:T(8,128)(2,1)S(1)}, bf16[160,512]{1,0:T(8,128)(2,1)S(1)}, u32[]{:S(2)}, u32[]{:S(2)}) collective-permute-start(bf16[160,512]{1,0:T(8,128)(2,1)S(1)} %get-tuple-element.434), channel_id=1, source_target_pairs={{1,0},{2,1},{3,2},{0,3},{5,4},{6,5},{7,6},{4,7},{9,8},{10,9},{11,1... | collective-permute-start | bytes 491528 | tf_op jit(solution)/shard_map/cond/branch_7_fun/ppermute | solution.py:350
  19.9 1.5 %collective-permute-start.35 = (bf16[104,512]{1,0:T(8,128)(2,1)S(1)}, bf16[104,512]{1,0:T(8,128)(2,1)S(1)}, u32[]{:S(2)}, u32[]{:S(2)}) collective-permute-start(bf16[104,512]{1,0:T(8,128)(2,1)S(1)} %slice.127), channel_id=1, source_target_pairs={{5,0},{6,1},{7,2},{4,3},{9,4},{10,5},{11,6},{8,7},{13,8},{14,9},{1... | collective-permute-start | bytes 319496 | tf_op jit(solution)/shard_map/cond/branch_7_fun/ppermute | solution.py:351
  21.4 1.5 %branch_7_fun.3 = (bf16[576,512]{1,0:T(8,128)(2,1)S(1)}, bf16[576,512]{1,0:T(8,128)(2,1)}, bf16[176,512]{1,0:T(8,128)(2,1)S(1)}, bf16[576,1024]{1,0:T(8,128)(2,1)S(1)}) custom-call(s32[8]{0:T(128)S(4)} %get-tuple-element.436.flags_ref, f32[32,128]{1,0:T(8,128)S(1)} %get-tuple-element.437.rows_ref, bf16[576,512]{1,0:T(8,128)(2,1)S(1)} %get-tuple-element.438.fine_ref, ...), custom_call_target="tpu_custom_call" | custom-call | flops 268435456 | bytes 4194304 | tf_op jit(solution)/shard_map/cond/branch_7_fun/pallas_call | solution.py:275
  23.0 2.6 %collective-permute-done.35.refs_2_ = bf16[104,512]{1,0:T(8,128)(2,1)S(1)} collective-permute-done((bf16[104,512]{1,0:T(8,128)(2,1)S(1)}, bf16[104,512]{1,0:T(8,128)(2,1)S(1)}, u32[]{:S(2)}, u32[]{:S(2)}) %collective-permute-start.35) | collective-permute-done | bytes 106528 | tf_op jit(solution)/shard_map/cond/branch_7_fun/ppermute | solution.py:351
  25.6 0.0 collective-permute-done.33.refs_0_
  25.6 0.5 %collective-permute-done.34.refs_1_ = bf16[160,512]{1,0:T(8,128)(2,1)S(1)} collective-permute-done((bf16[160,512]{1,0:T(8,128)(2,1)S(1)}, bf16[160,512]{1,0:T(8,128)(2,1)S(1)}, u32[]{:S(2)}, u32[]{:S(2)}) %collective-permute-start.34) | collective-permute-done | bytes 163872 | tf_op jit(solution)/shard_map/cond/branch_7_fun/ppermute | solution.py:350
  26.1 5.0 %shard_map.120 = (bf16[144,1024]{1,0:T(8,128)(2,1)S(1)}, bf16[128,512]{1,0:T(8,128)(2,1)S(1)}, bf16[128,512]{1,0:T(8,128)(2,1)S(1)}, bf16[88,512]{1,0:T(8,128)(2,1)S(1)}) custom-call(s32[8]{0:T(128)S(4)} %get-tuple-element.532.flags_ref, bf16[2048,1024]{1,0:T(8,128)(2,1)} %merge_hbm.1, bf16[1024,1536]{1,0:T(8,128)(2,1)} %qkv_w_hbm.3, ...), custom_call_target="tpu_custom_call" | custom-call | flops 3221225472 | bytes 12582912 | tf_op jit(solution)/shard_map/pallas_call | solution.py:275
  31.1 8.9 %conditional.5 = (bf16[2,12,24,512]{3,2,1,0:T(8,128)(2,1)}, bf16[2,6,12,1024]{3,0,2,1:T(2,128)(2,1)}) conditional(s32[]{:T(128)S(4)} %bitcast.12, (bf16[576,512]{1,0:T(8,128)(2,1)}, bf16[432,512]{1,0:T(8,128)(2,1)S(1)}, f32[32,128]{1,0:T(8,128)S(1)}, bf16[128,512]{1,0:T(8,128)(2,1)S(1)}, ...), branch_computations={%region_13.0_spmd, %region_14.0_spmd, %region_15.0_spmd, %region_1... | conditional | flops 1342177280 | bytes 6865032 | solution.py:368
  31.1 1.0 %collective-permute-start.44 = (bf16[32,512]{1,0:T(8,128)(2,1)S(1)}, bf16[32,512]{1,0:T(8,128)(2,1)S(1)}, u32[]{:S(2)}, u32[]{:S(2)}) collective-permute-start(bf16[32,512]{1,0:T(8,128)(2,1)S(1)} %slice.136), channel_id=1, source_target_pairs={{31,0},{28,1},{29,2},{30,3},{3,4},{0,5},{1,6},{2,7},{7,8},{4,9},{5... | collective-permute-start | bytes 98312 | tf_op jit(solution)/shard_map/cond/branch_2_fun/ppermute | solution.py:351
  32.1 1.3 %collective-permute-start.43 = (bf16[64,512]{1,0:T(8,128)(2,1)S(1)}, bf16[64,512]{1,0:T(8,128)(2,1)S(1)}, u32[]{:S(2)}, u32[]{:S(2)}) collective-permute-start(bf16[64,512]{1,0:T(8,128)(2,1)S(1)} %slice.135), channel_id=1, source_target_pairs={{3,0},{0,1},{1,2},{2,3},{7,4},{4,5},{5,6},{6,7},{11,8},{8,9},{9,10... | collective-permute-start | bytes 196616 | tf_op jit(solution)/shard_map/cond/branch_2_fun/ppermute | solution.py:350
  33.3 0.0 collective-permute-start.42
  33.4 2.5 %branch_2_fun.10 = bf16[2,12,24,512]{3,2,1,0:T(8,128)(2,1)} custom-call(bf16[576,512]{1,0:T(8,128)(2,1)} %get-tuple-element.458.part_hbm, bf16[432,512]{1,0:T(8,128)(2,1)S(1)} %get-tuple-element.459.source_ref, f32[32,128]{1,0:T(8,128)S(1)} %get-tuple-element.460.rows_ref.refs_3_), custom_call_target="tpu_custom_call" | custom-call | flops 1073741824 | bytes 4194304 | tf_op jit(solution)/shard_map/cond/branch_2_fun/pallas_call | solution.py:275
  35.8 2.4 %collective-permute-done.44.refs_2_ = bf16[32,512]{1,0:T(8,128)(2,1)S(1)} collective-permute-done((bf16[32,512]{1,0:T(8,128)(2,1)S(1)}, bf16[32,512]{1,0:T(8,128)(2,1)S(1)}, u32[]{:S(2)}, u32[]{:S(2)}) %collective-permute-start.44) | collective-permute-done | bytes 32800 | tf_op jit(solution)/shard_map/cond/branch_2_fun/ppermute | solution.py:351
  38.2 0.4 collective-permute-done.43.refs_1_
  38.6 0.0 collective-permute-done.42.refs_0_
  38.6 1.1 %branch_2_fun.11 = bf16[6,12,2,1024]{3,2,1,0:T(2,128)(2,1)} custom-call(bf16[144,1024]{1,0:T(8,128)(2,1)S(1)} %get-tuple-element.461.coarse_ref, bf16[64,512]{1,0:T(8,128)(2,1)S(1)} %collective-permute-done.42.refs_0_, bf16[64,512]{1,0:T(8,128)(2,1)S(1)} %collective-permute-done.43.refs_1_, bf16[32,512]{1,0:T(8,128)(2,1)S(1)} %collective-permute-done.44.refs_2_, ...), custom_call_target="tpu_custom_call" | custom-call | flops 268435456 | bytes 1048576 | tf_op jit(solution)/shard_map/cond/branch_2_fun/pallas_call | solution.py:275
  (9 shorter events, 0.1 us)
Async XLA Ops:
  2.2 9.8 %collective-permute-start.1 = (bf16[48,512]{1,0:T(8,128)(2,1)S(1)}, bf16[48,512]{1,0:T(8,128)(2,1)S(1)}, u32[]{:S(2)}, u32[]{:S(2)}) collective-permute-start(bf16[48,512]{1,0:T(8,128)(2,1)S(1)} %slice.97), channel_id=1, source_target_pairs={{3,0},{0,1},{1,2},{2,3},{7,4},{4,5},{5,6},{6,7},{11,8},{8,9},{9,10... | collective-permute-start | bytes 147464 | tf_op jit(solution)/shard_map/cond/branch_0_fun/ppermute | solution.py:350
  5.3 6.7 %collective-permute-start = (bf16[48,512]{1,0:T(8,128)(2,1)S(1)}, bf16[48,512]{1,0:T(8,128)(2,1)S(1)}, u32[]{:S(2)}, u32[]{:S(2)}) collective-permute-start(bf16[48,512]{1,0:T(8,128)(2,1)S(1)} %slice.96), channel_id=1, source_target_pairs={{28,0},{0,4},{4,8},{8,12},{12,16},{16,20},{20,24},{24,28},{29,1},{... | collective-permute-start | bytes 147464 | tf_op jit(solution)/shard_map/cond/branch_0_fun/ppermute | solution.py:352
  5.3 6.7 %collective-permute-start.2 = (bf16[8,512]{1,0:T(8,128)(2,1)S(1)}, bf16[8,512]{1,0:T(8,128)(2,1)S(1)}, u32[]{:S(2)}, u32[]{:S(2)}) collective-permute-start(bf16[8,512]{1,0:T(8,128)(2,1)S(1)} %slice.98), channel_id=1, source_target_pairs={{31,0},{28,1},{29,2},{30,3},{3,4},{0,5},{1,6},{2,7},{7,8},{4,9},{5... | collective-permute-start | bytes 24584 | tf_op jit(solution)/shard_map/cond/branch_0_fun/ppermute | solution.py:351
  18.2 7.3 %collective-permute-start.33 = (bf16[160,512]{1,0:T(8,128)(2,1)S(1)}, bf16[160,512]{1,0:T(8,128)(2,1)S(1)}, u32[]{:S(2)}, u32[]{:S(2)}) collective-permute-start(bf16[160,512]{1,0:T(8,128)(2,1)S(1)} %get-tuple-element.433), channel_id=1, source_target_pairs={{4,0},{8,4},{12,8},{16,12},{20,16},{24,20},{28,24},{0,28},{5,1},{9... | collective-permute-start | bytes 491528 | tf_op jit(solution)/shard_map/cond/branch_7_fun/ppermute | solution.py:352
  19.4 6.6 %collective-permute-start.34 = (bf16[160,512]{1,0:T(8,128)(2,1)S(1)}, bf16[160,512]{1,0:T(8,128)(2,1)S(1)}, u32[]{:S(2)}, u32[]{:S(2)}) collective-permute-start(bf16[160,512]{1,0:T(8,128)(2,1)S(1)} %get-tuple-element.434), channel_id=1, source_target_pairs={{1,0},{2,1},{3,2},{0,3},{5,4},{6,5},{7,6},{4,7},{9,8},{10,9},{11,1... | collective-permute-start | bytes 491528 | tf_op jit(solution)/shard_map/cond/branch_7_fun/ppermute | solution.py:350
  19.9 5.6 %collective-permute-start.35 = (bf16[104,512]{1,0:T(8,128)(2,1)S(1)}, bf16[104,512]{1,0:T(8,128)(2,1)S(1)}, u32[]{:S(2)}, u32[]{:S(2)}) collective-permute-start(bf16[104,512]{1,0:T(8,128)(2,1)S(1)} %slice.127), channel_id=1, source_target_pairs={{5,0},{6,1},{7,2},{4,3},{9,4},{10,5},{11,6},{8,7},{13,8},{14,9},{1... | collective-permute-start | bytes 319496 | tf_op jit(solution)/shard_map/cond/branch_7_fun/ppermute | solution.py:351
  31.1 7.1 %collective-permute-start.44 = (bf16[32,512]{1,0:T(8,128)(2,1)S(1)}, bf16[32,512]{1,0:T(8,128)(2,1)S(1)}, u32[]{:S(2)}, u32[]{:S(2)}) collective-permute-start(bf16[32,512]{1,0:T(8,128)(2,1)S(1)} %slice.136), channel_id=1, source_target_pairs={{31,0},{28,1},{29,2},{30,3},{3,4},{0,5},{1,6},{2,7},{7,8},{4,9},{5... | collective-permute-start | bytes 98312 | tf_op jit(solution)/shard_map/cond/branch_2_fun/ppermute | solution.py:351
  32.1 6.5 %collective-permute-start.43 = (bf16[64,512]{1,0:T(8,128)(2,1)S(1)}, bf16[64,512]{1,0:T(8,128)(2,1)S(1)}, u32[]{:S(2)}, u32[]{:S(2)}) collective-permute-start(bf16[64,512]{1,0:T(8,128)(2,1)S(1)} %slice.135), channel_id=1, source_target_pairs={{3,0},{0,1},{1,2},{2,3},{7,4},{4,5},{5,6},{6,7},{11,8},{8,9},{9,10... | collective-permute-start | bytes 196616 | tf_op jit(solution)/shard_map/cond/branch_2_fun/ppermute | solution.py:350
  33.3 5.3 %collective-permute-start.42 = (bf16[64,512]{1,0:T(8,128)(2,1)S(1)}, bf16[64,512]{1,0:T(8,128)(2,1)S(1)}, u32[]{:S(2)}, u32[]{:S(2)}) collective-permute-start(bf16[64,512]{1,0:T(8,128)(2,1)S(1)} %slice.134), channel_id=1, source_target_pairs={{28,0},{0,4},{4,8},{8,12},{12,16},{16,20},{20,24},{24,28},{29,1},{... | collective-permute-start | bytes 196616 | tf_op jit(solution)/shard_map/cond/branch_2_fun/ppermute | solution.py:352

commit v3 on v0

--- a/solution.py
+++ b/solution.py
@@ -106,7 +106,7 @@
             come = 1 if a > 0 else -1
             one = exchange_places(block, fine, rows, cols, come)
             home = [p for p in block if p not in set(fine)]
-            wanted = quarters + (home if come == -ahead and 2 * big_a != a else [])
+            wanted = quarters + (home if come == -ahead and abs(2 * big_a - a) >= abs(a) else [])
             two = exchange_places(fine, wanted, rows, cols, ahead)
             back = 1 if big_a < 0 else -1
             three = exchange_places(coarse, cblock, crows, ccols, back)
@@ -473,7 +473,7 @@
 
 def before_coarse(flags, fine, table, weight, plan):
     own, width = fine.shape
-    half = 9 * weight.shape[0] // 32
+    half = weight.shape[0] // 4
 
     def body(flags_ref, rows_ref, fine_ref, weight_hbm, x_ref, part_hbm, home_ref, weight_ref, part_ref, sems):
         start = Copies(sems)

time: 40.4 us -> 40.1 us (level)
  starting transfers between devices: 14 us -> 10.3 us
  waiting for transfers between devices: 6.38 us -> 9.17 us
    ppermute x3, starting transfers between devices: 8.32 us -> 1.65 us  [exchange(): both = lax.ppermute(both, ('lat', 'lon'), pairs)]
    ppermute x3, waiting for transfers between devices: 5.13 us -> 8.17 us  [exchange(): both = lax.ppermute(both, ('lat', 'lon'), pairs)]
    ppermute x3, starting transfers between devices: 4.37 us -> 6.84 us  [exchange(): col = lax.ppermute(col, 'lon', [((j + sign) % lon, j) for j in range(lon)])]
    ppermute x3, starting transfers between devices: 1.28 us -> 1.87 us  [exchange(): row = lax.ppermute(row, 'lat', [((i + sign) % lat, i) for i in range(lat)])]
where the time goes in v3:
time: 40.1 us; the launch traced here: 40.5 us
  Pallas kernels  19.4 us (48%)
  starting transfers between devices  10.3 us (26%)
  waiting for transfers between devices  9.17 us (23%)
  between operations  0.87 us (2%)
  loops' own time  0.72 us (2%)
    pallas_call x9, Pallas kernels, call(): pl.pallas_call(body, out_shape=outs, in_specs=in_specs, out_specs=out_spe...  19.4 us
    ppermute x3, waiting for transfers between devices, exchange(): both = lax.ppermute(both, ('lat', 'lon'), pairs)  8.17 us
    ppermute x3, starting transfers between devices, exchange(): col = lax.ppermute(col, 'lon', [((j + sign) % lon, j) for j in range(lon)])  6.84 us
    ppermute x3, starting transfers between devices, exchange(): row = lax.ppermute(row, 'lat', [((i + sign) % lat, i) for i in range(lat)])  1.87 us
    ppermute x3, starting transfers between devices, exchange(): both = lax.ppermute(both, ('lat', 'lon'), pairs)  1.65 us
    ppermute x3, waiting for transfers between devices, exchange(): col = lax.ppermute(col, 'lon', [((j + sign) % lon, j) for j in range(lon)])  0.99 us
  transfers between devices with their start and end apart: 9, of which 3 were waited for; matrix products, arithmetic and copies ran while one was open for 0% of the time, Pallas kernels for 14%

profile of v3, /device:TPU:0, one launch (start us, length us, event | category | flops | bytes accessed | tf_op | source)
XLA Modules:
  0.0 40.5 jit_solution(12610566635085506888)
XLA Ops:
  0.6 1.6 %shard_map.120 = (bf16[112,512]{1,0:T(8,128)(2,1)S(1)}, bf16[112,512]{1,0:T(8,128)(2,1)S(1)}, bf16[48,512]{1,0:T(8,128)(2,1)S(1)}, bf16[576,512]{1,0:T(8,128)(2,...) custom-call(s32[2]{0:T(128)} %shifts_hbm.1, ...), custom_call_target="tpu_custom_call" | custom-call | flops 268435456 | bytes 1048576 | tf_op jit(solution)/shard_map/pallas_call | solution.py:275
  2.2 10.0 %conditional.3 = (bf16[272,512]{1,0:T(8,128)(2,1)S(1)}, f32[7,128]{1,0:T(8,128)S(1)}, bf16[576,512]{1,0:T(8,128)(2,1)S(1)}, bf16[512,1024]{1,0:T(8,128)(2,1)S(1)}, bf16[512,512]{1,0:T(8,128)(2,1)S(1)}) conditional(s32[]{:T(128)S(4)} %bitcast.15, (bf16[112,512]{1,0:T(8,128)(2,1)S(1)}, bf16[112,512]{1,0:T(8,128)(2,1)S(1)}, ...), branch_computations={%region_0.0_spmd, %region_1.0_spmd, %region_2.0_spmd, %region_3.0_... | conditional | flops 268435456 | bytes 5619872 | solution.py:368
  2.3 5.1 %collective-permute-start.10 = (bf16[80,512]{1,0:T(8,128)(2,1)S(1)}, bf16[80,512]{1,0:T(8,128)(2,1)S(1)}, u32[]{:S(2)}, u32[]{:S(2)}) collective-permute-start(bf16[80,512]{1,0:T(8,128)(2,1)S(1)} %slice.108), channel_id=1, source_target_pairs={{1,0},{2,1},{3,2},{0,3},{5,4},{6,5},{7,6},{4,7},{9,8},{10,9},{11,1... | collective-permute-start | bytes 245768 | tf_op jit(solution)/shard_map/cond/branch_3_fun/ppermute | solution.py:350
  7.4 1.6 %collective-permute-start.9 = (bf16[80,512]{1,0:T(8,128)(2,1)S(1)}, bf16[80,512]{1,0:T(8,128)(2,1)S(1)}, u32[]{:S(2)}, u32[]{:S(2)}) collective-permute-start(bf16[80,512]{1,0:T(8,128)(2,1)S(1)} %slice.107), channel_id=1, source_target_pairs={{4,0},{8,4},{12,8},{16,12},{20,16},{24,20},{28,24},{0,28},{5,1},{9... | collective-permute-start | bytes 245768 | tf_op jit(solution)/shard_map/cond/branch_3_fun/ppermute | solution.py:352
  9.0 0.8 %collective-permute-start.11 = (bf16[16,512]{1,0:T(8,128)(2,1)S(1)}, bf16[16,512]{1,0:T(8,128)(2,1)S(1)}, u32[]{:S(2)}, u32[]{:S(2)}) collective-permute-start(bf16[16,512]{1,0:T(8,128)(2,1)S(1)} %slice.109), channel_id=1, source_target_pairs={{5,0},{6,1},{7,2},{4,3},{9,4},{10,5},{11,6},{8,7},{13,8},{14,9},{1... | collective-permute-start | bytes 49160 | tf_op jit(solution)/shard_map/cond/branch_3_fun/ppermute | solution.py:351
  9.8 1.7 %branch_3_fun.7 = (f32[7,128]{1,0:T(8,128)S(1)}, bf16[576,512]{1,0:T(8,128)(2,1)S(1)}, bf16[512,1024]{1,0:T(8,128)(2,1)S(1)}, bf16[512,512]{1,0:T(8,128)(2,1)S(1)}) custom-call(s32[8]{0:T(128)S(4)} %get-tuple-element.350.flags_ref, f32[32,128]{1,0:T(8,128)S(1)} %get-tuple-element.351.rows_ref, bf16[576,512]{1,0:T(8,128)(2,1)S(1)} %get-tuple-element.352.tokens_ref, ...), custom_call_target="tpu_custom_call" | custom-call | flops 268435456 | bytes 4194304 | tf_op jit(solution)/shard_map/cond/branch_3_fun/pallas_call | solution.py:275
  11.5 0.6 %collective-permute-done.11.refs_2_ = bf16[16,512]{1,0:T(8,128)(2,1)S(1)} collective-permute-done((bf16[16,512]{1,0:T(8,128)(2,1)S(1)}, bf16[16,512]{1,0:T(8,128)(2,1)S(1)}, u32[]{:S(2)}, u32[]{:S(2)}) %collective-permute-start.11) | collective-permute-done | bytes 16416 | tf_op jit(solution)/shard_map/cond/branch_3_fun/ppermute | solution.py:351
  12.1 0.0 collective-permute-done.10.refs_1_
  12.1 0.0 collective-permute-done.9.refs_0_
  12.2 5.9 %shard_map.121 = (bf16[576,512]{1,0:T(8,128)(2,1)S(1)}, bf16[160,512]{1,0:T(8,128)(2,1)S(1)}, bf16[160,512]{1,0:T(8,128)(2,1)S(1)}, bf16[112,512]{1,0:T(8,128)(2,1)S(1)}) custom-call(bf16[576,512]{1,0:T(8,128)(2,1)S(1)} %get-tuple-element.562.own_ref, bf16[272,512]{1,0:T(8,128)(2,1)S(1)} %get-tuple-element.563.source_ref, ...), custom_call_target="tpu_custom_call" | custom-call | flops 3221225472 | bytes 6291456 | tf_op jit(solution)/shard_map/pallas_call | solution.py:275
  18.1 10.6 %conditional.4 = (bf16[432,512]{1,0:T(8,128)(2,1)S(1)}, bf16[576,512]{1,0:T(8,128)(2,1)S(1)}, bf16[576,512]{1,0:T(8,128)(2,1)}, bf16[192,512]{1,0:T(8,128)(2,1)S(1)}, bf16[512,1024]{1,0:T(8,128)(2,1)S(1)}) conditional(s32[]{:T(128)S(4)} %bitcast.14, (s32[8]{0:T(128)S(4)}, f32[32,128]{1,0:T(8,128)S(1)}, ...), branch_computations={%region_5.0_spmd, %region_6.0_spmd, %region_7.0_spmd, %region_8.0_... | conditional | flops 268435456 | bytes 6619296 | solution.py:368
  18.4 1.0 %collective-permute-start.28 = (bf16[144,512]{1,0:T(8,128)(2,1)S(1)}, bf16[144,512]{1,0:T(8,128)(2,1)S(1)}, u32[]{:S(2)}, u32[]{:S(2)}) collective-permute-start(bf16[144,512]{1,0:T(8,128)(2,1)S(1)} %slice.124), channel_id=1, source_target_pairs={{3,0},{0,1},{1,2},{2,3},{7,4},{4,5},{5,6},{6,7},{11,8},{8,9},{9,10... | collective-permute-start | bytes 442376 | tf_op jit(solution)/shard_map/cond/branch_5_fun/ppermute | solution.py:350
  19.4 0.1 collective-permute-start.27
  19.5 0.1 collective-permute-start.29
  19.6 1.5 %branch_5_fun.5 = (bf16[576,512]{1,0:T(8,128)(2,1)S(1)}, bf16[576,512]{1,0:T(8,128)(2,1)}, bf16[192,512]{1,0:T(8,128)(2,1)S(1)}, bf16[512,1024]{1,0:T(8,128)(2,1)S(1)}) custom-call(s32[8]{0:T(128)S(4)} %get-tuple-element.428.flags_ref, f32[32,128]{1,0:T(8,128)S(1)} %get-tuple-element.429.rows_ref, bf16[576,512]{1,0:T(8,128)(2,1)S(1)} %get-tuple-element.430.fine_ref, ...), custom_call_target="tpu_custom_call" | custom-call | flops 268435456 | bytes 4194304 | tf_op jit(solution)/shard_map/cond/branch_5_fun/pallas_call | solution.py:275
  21.1 7.6 %collective-permute-done.29.refs_2_ = bf16[64,512]{1,0:T(8,128)(2,1)S(1)} collective-permute-done((bf16[64,512]{1,0:T(8,128)(2,1)S(1)}, bf16[64,512]{1,0:T(8,128)(2,1)S(1)}, u32[]{:S(2)}, u32[]{:S(2)}) %collective-permute-start.29) | collective-permute-done | bytes 65568 | tf_op jit(solution)/shard_map/cond/branch_5_fun/ppermute | solution.py:351
  28.7 0.0 collective-permute-done.28.refs_1_
  28.7 0.0 collective-permute-done.27.refs_0_
  28.7 5.0 %shard_map.122 = (bf16[144,1024]{1,0:T(8,128)(2,1)S(1)}, bf16[128,512]{1,0:T(8,128)(2,1)S(1)}, bf16[128,512]{1,0:T(8,128)(2,1)S(1)}, bf16[88,512]{1,0:T(8,128)(2,1)S(1)}) custom-call(s32[8]{0:T(128)S(4)} %get-tuple-element.555.flags_ref, bf16[2048,1024]{1,0:T(8,128)(2,1)} %merge_hbm.1, bf16[1024,1536]{1,0:T(8,128)(2,1)} %qkv_w_hbm.3, ...), custom_call_target="tpu_custom_call" | custom-call | flops 3221225472 | bytes 12582912 | tf_op jit(solution)/shard_map/pallas_call | solution.py:275
  33.8 6.6 %conditional.5 = (bf16[2,12,24,512]{3,2,1,0:T(8,128)(2,1)}, bf16[2,6,12,1024]{3,0,2,1:T(2,128)(2,1)}) conditional(s32[]{:T(128)S(4)} %bitcast.13, (bf16[576,512]{1,0:T(8,128)(2,1)}, bf16[432,512]{1,0:T(8,128)(2,1)S(1)}, f32[32,128]{1,0:T(8,128)S(1)}, bf16[128,512]{1,0:T(8,128)(2,1)S(1)}, ...), branch_computations={%region_13.0_spmd, %region_14.0_spmd, %region_15.0_spmd, %region_1... | conditional | flops 1342177280 | bytes 7012488 | solution.py:368
  33.8 0.7 %collective-permute-start.41 = (bf16[16,512]{1,0:T(8,128)(2,1)S(1)}, bf16[16,512]{1,0:T(8,128)(2,1)S(1)}, u32[]{:S(2)}, u32[]{:S(2)}) collective-permute-start(bf16[16,512]{1,0:T(8,128)(2,1)S(1)} %slice.133), channel_id=1, source_target_pairs={{5,0},{6,1},{7,2},{4,3},{9,4},{10,5},{11,6},{8,7},{13,8},{14,9},{1... | collective-permute-start | bytes 49160 | tf_op jit(solution)/shard_map/cond/branch_1_fun/ppermute | solution.py:351
  34.6 0.7 %collective-permute-start.40 = (bf16[48,512]{1,0:T(8,128)(2,1)S(1)}, bf16[48,512]{1,0:T(8,128)(2,1)S(1)}, u32[]{:S(2)}, u32[]{:S(2)}) collective-permute-start(bf16[48,512]{1,0:T(8,128)(2,1)S(1)} %slice.132), channel_id=1, source_target_pairs={{1,0},{2,1},{3,2},{0,3},{5,4},{6,5},{7,6},{4,7},{9,8},{10,9},{11,1... | collective-permute-start | bytes 147464 | tf_op jit(solution)/shard_map/cond/branch_1_fun/ppermute | solution.py:350
  35.3 0.2 collective-permute-start.39
  35.5 2.5 %branch_1_fun.10 = bf16[2,12,24,512]{3,2,1,0:T(8,128)(2,1)} custom-call(bf16[576,512]{1,0:T(8,128)(2,1)} %get-tuple-element.465.part_hbm, bf16[432,512]{1,0:T(8,128)(2,1)S(1)} %get-tuple-element.466.source_ref, f32[32,128]{1,0:T(8,128)S(1)} %get-tuple-element.467.rows_ref.refs_3_), custom_call_target="tpu_custom_call" | custom-call | flops 1073741824 | bytes 4194304 | tf_op jit(solution)/shard_map/cond/branch_1_fun/pallas_call | solution.py:275
  37.9 0.0 collective-permute-done.41.refs_2_
  38.0 1.0 %collective-permute-done.40.refs_1_ = bf16[48,512]{1,0:T(8,128)(2,1)S(1)} collective-permute-done((bf16[48,512]{1,0:T(8,128)(2,1)S(1)}, bf16[48,512]{1,0:T(8,128)(2,1)S(1)}, u32[]{:S(2)}, u32[]{:S(2)}) %collective-permute-start.40) | collective-permute-done | bytes 49184 | tf_op jit(solution)/shard_map/cond/branch_1_fun/ppermute | solution.py:350
  38.9 0.0 collective-permute-done.39.refs_0_
  38.9 1.1 %branch_1_fun.11 = bf16[6,12,2,1024]{3,2,1,0:T(2,128)(2,1)} custom-call(bf16[144,1024]{1,0:T(8,128)(2,1)S(1)} %get-tuple-element.468.coarse_ref, bf16[48,512]{1,0:T(8,128)(2,1)S(1)} %collective-permute-done.39.refs_0_, bf16[48,512]{1,0:T(8,128)(2,1)S(1)} %collective-permute-done.40.refs_1_, bf16[16,512]{1,0:T(8,128)(2,1)S(1)} %collective-permute-done.41.refs_2_, ...), custom_call_target="tpu_custom_call" | custom-call | flops 268435456 | bytes 1048576 | tf_op jit(solution)/shard_map/cond/branch_1_fun/pallas_call | solution.py:275
  (11 shorter events, 0.1 us)
Async XLA Ops:
  2.3 9.9 %collective-permute-start.10 = (bf16[80,512]{1,0:T(8,128)(2,1)S(1)}, bf16[80,512]{1,0:T(8,128)(2,1)S(1)}, u32[]{:S(2)}, u32[]{:S(2)}) collective-permute-start(bf16[80,512]{1,0:T(8,128)(2,1)S(1)} %slice.108), channel_id=1, source_target_pairs={{1,0},{2,1},{3,2},{0,3},{5,4},{6,5},{7,6},{4,7},{9,8},{10,9},{11,1... | collective-permute-start | bytes 245768 | tf_op jit(solution)/shard_map/cond/branch_3_fun/ppermute | solution.py:350
  7.4 4.8 %collective-permute-start.9 = (bf16[80,512]{1,0:T(8,128)(2,1)S(1)}, bf16[80,512]{1,0:T(8,128)(2,1)S(1)}, u32[]{:S(2)}, u32[]{:S(2)}) collective-permute-start(bf16[80,512]{1,0:T(8,128)(2,1)S(1)} %slice.107), channel_id=1, source_target_pairs={{4,0},{8,4},{12,8},{16,12},{20,16},{24,20},{28,24},{0,28},{5,1},{9... | collective-permute-start | bytes 245768 | tf_op jit(solution)/shard_map/cond/branch_3_fun/ppermute | solution.py:352
  9.0 3.2 %collective-permute-start.11 = (bf16[16,512]{1,0:T(8,128)(2,1)S(1)}, bf16[16,512]{1,0:T(8,128)(2,1)S(1)}, u32[]{:S(2)}, u32[]{:S(2)}) collective-permute-start(bf16[16,512]{1,0:T(8,128)(2,1)S(1)} %slice.109), channel_id=1, source_target_pairs={{5,0},{6,1},{7,2},{4,3},{9,4},{10,5},{11,6},{8,7},{13,8},{14,9},{1... | collective-permute-start | bytes 49160 | tf_op jit(solution)/shard_map/cond/branch_3_fun/ppermute | solution.py:351
  18.4 10.3 %collective-permute-start.28 = (bf16[144,512]{1,0:T(8,128)(2,1)S(1)}, bf16[144,512]{1,0:T(8,128)(2,1)S(1)}, u32[]{:S(2)}, u32[]{:S(2)}) collective-permute-start(bf16[144,512]{1,0:T(8,128)(2,1)S(1)} %slice.124), channel_id=1, source_target_pairs={{3,0},{0,1},{1,2},{2,3},{7,4},{4,5},{5,6},{6,7},{11,8},{8,9},{9,10... | collective-permute-start | bytes 442376 | tf_op jit(solution)/shard_map/cond/branch_5_fun/ppermute | solution.py:350
  19.4 9.3 %collective-permute-start.27 = (bf16[144,512]{1,0:T(8,128)(2,1)S(1)}, bf16[144,512]{1,0:T(8,128)(2,1)S(1)}, u32[]{:S(2)}, u32[]{:S(2)}) collective-permute-start(bf16[144,512]{1,0:T(8,128)(2,1)S(1)} %slice.123), channel_id=1, source_target_pairs={{28,0},{0,4},{4,8},{8,12},{12,16},{16,20},{20,24},{24,28},{29,1},{... | collective-permute-start | bytes 442376 | tf_op jit(solution)/shard_map/cond/branch_5_fun/ppermute | solution.py:352
  19.5 9.2 %collective-permute-start.29 = (bf16[64,512]{1,0:T(8,128)(2,1)S(1)}, bf16[64,512]{1,0:T(8,128)(2,1)S(1)}, u32[]{:S(2)}, u32[]{:S(2)}) collective-permute-start(bf16[64,512]{1,0:T(8,128)(2,1)S(1)} %slice.125), channel_id=1, source_target_pairs={{31,0},{28,1},{29,2},{30,3},{3,4},{0,5},{1,6},{2,7},{7,8},{4,9},{5... | collective-permute-start | bytes 196616 | tf_op jit(solution)/shard_map/cond/branch_5_fun/ppermute | solution.py:351
  33.8 4.1 %collective-permute-start.41 = (bf16[16,512]{1,0:T(8,128)(2,1)S(1)}, bf16[16,512]{1,0:T(8,128)(2,1)S(1)}, u32[]{:S(2)}, u32[]{:S(2)}) collective-permute-start(bf16[16,512]{1,0:T(8,128)(2,1)S(1)} %slice.133), channel_id=1, source_target_pairs={{5,0},{6,1},{7,2},{4,3},{9,4},{10,5},{11,6},{8,7},{13,8},{14,9},{1... | collective-permute-start | bytes 49160 | tf_op jit(solution)/shard_map/cond/branch_1_fun/ppermute | solution.py:351
  34.6 4.4 %collective-permute-start.40 = (bf16[48,512]{1,0:T(8,128)(2,1)S(1)}, bf16[48,512]{1,0:T(8,128)(2,1)S(1)}, u32[]{:S(2)}, u32[]{:S(2)}) collective-permute-start(bf16[48,512]{1,0:T(8,128)(2,1)S(1)} %slice.132), channel_id=1, source_target_pairs={{1,0},{2,1},{3,2},{0,3},{5,4},{6,5},{7,6},{4,7},{9,8},{10,9},{11,1... | collective-permute-start | bytes 147464 | tf_op jit(solution)/shard_map/cond/branch_1_fun/ppermute | solution.py:350
  35.3 3.7 %collective-permute-start.39 = (bf16[48,512]{1,0:T(8,128)(2,1)S(1)}, bf16[48,512]{1,0:T(8,128)(2,1)S(1)}, u32[]{:S(2)}, u32[]{:S(2)}) collective-permute-start(bf16[48,512]{1,0:T(8,128)(2,1)S(1)} %slice.131), channel_id=1, source_target_pairs={{4,0},{8,4},{12,8},{16,12},{20,16},{24,20},{28,24},{0,28},{5,1},{9... | collective-permute-start | bytes 147464 | tf_op jit(solution)/shard_map/cond/branch_1_fun/ppermute | solution.py:352
